TPU v7x, 128 devices: a whole 4x4x4 slice. The times are simulated.
128 devices in a mesh: row: 16 (over z_hi, y, core), col: 8 (over z_lo, x).
Axes of the slice: x: 4, y: 4, z: 4 (z_hi: 2, z_lo: 2; z = z_hi * 2 + z_lo), core: 2. Of those that a mesh axis runs over, the one named last changes fastest.
Arguments:
- pair_rep: bfloat16 [320, 320, 128], P('row', 'col'), may hold values from -6 to 6
- proj_weight: bfloat16 [2, 128, 512], replicated, may hold values from -0.5 to 0.5
- gate_weight: bfloat16 [2, 128, 128], replicated, may hold values from -0.5 to 0.5
- out_weight: bfloat16 [2, 128, 128], replicated, may hold values from -0.5 to 0.5
- pair_cot: bfloat16 [320, 320, 128], P('row', 'col'), may hold values from -6 to 6
Outputs:
- pair_out: bfloat16 [320, 320, 128], P('row', 'col')
- pair_grad: float32 [320, 320, 128], P('row', 'col')
- proj_grad: float32 [2, 128, 512], replicated
- gate_grad: float32 [2, 128, 128], replicated
- out_grad: float32 [2, 128, 128], replicated
All inputs are finite; a program needn't handle non-finite values.
Results may differ from a plain program's by a relative error of at most 0.034.
Values may be sent and summed in bfloat16 or wider, within the bound.
No kernel may reach another device: no remote copies, remote signals or barrier semaphores. Data moves between devices by JAX's collectives and lax.ppermute only.
A program may use at most 128 MiB of HBM per device.

v0:
```python
import jax
import jax.numpy as jnp
from jax import lax
from jax.sharding import PartitionSpec as P

EPSILON = 1e-05


def layer_norm(values):
    centered = values - jnp.mean(values, axis=-1, keepdims=True)
    inverse = lax.rsqrt(jnp.mean(centered * centered, axis=-1, keepdims=True) + EPSILON)
    return centered * inverse


def norm_back(values, upstream):
    centered = values - jnp.mean(values, axis=-1, keepdims=True)
    inverse = lax.rsqrt(jnp.mean(centered * centered, axis=-1, keepdims=True) + EPSILON)
    normed = centered * inverse
    mean_up = jnp.mean(upstream, axis=-1, keepdims=True)
    mean_cross = jnp.mean(upstream * normed, axis=-1, keepdims=True)
    return inverse * (upstream - mean_up - normed * mean_cross)


def contract(pattern, first_op, second_op):
    return jnp.einsum(pattern, first_op, second_op, preferred_element_type=jnp.float32)


def project(pair_rep, proj_mat, gate_mat):
    pair_full = pair_rep.astype(jnp.float32)
    normed = layer_norm(pair_full).astype(jnp.bfloat16)
    projected = contract("ijc,ch->ijh", normed, proj_mat)
    hidden = proj_mat.shape[1] // 4
    left_side = (
        jax.nn.sigmoid(projected[..., :hidden]) * projected[..., hidden : 2 * hidden]
    ).astype(jnp.bfloat16)
    right_side = (
        jax.nn.sigmoid(projected[..., 2 * hidden : 3 * hidden]) * projected[..., 3 * hidden :]
    ).astype(jnp.bfloat16)
    gating = jax.nn.sigmoid(contract("ijc,cd->ijd", normed, gate_mat))
    return (pair_full, normed, projected, left_side, right_side, gating)


def finish(pair_full, mix_value, out_mat, gating):
    normed_mix = layer_norm(mix_value).astype(jnp.bfloat16)
    product = contract("ijh,hc->ijc", normed_mix, out_mat)
    return ((pair_full + gating * product).astype(jnp.bfloat16), normed_mix, product)


def back_head(upstream, gating, product, normed_mix, mix_value, out_mat):
    through = (upstream * gating).astype(jnp.bfloat16)
    gate_pre = upstream * product * gating * (1.0 - gating)
    mix_up = contract("ijc,hc->ijh", through, out_mat)
    out_part = contract("ijh,ijc->hc", normed_mix, through)
    mix_grad = norm_back(mix_value, mix_up).astype(jnp.bfloat16)
    return (mix_grad, out_part, gate_pre)


def back_tail(
    upstream, pair_full, normed, projected, left_grad, right_grad, gate_pre, proj_mat, gate_mat
):
    hidden = proj_mat.shape[1] // 4
    left_gate = jax.nn.sigmoid(projected[..., :hidden])
    left_value = projected[..., hidden : 2 * hidden]
    right_gate = jax.nn.sigmoid(projected[..., 2 * hidden : 3 * hidden])
    right_value = projected[..., 3 * hidden :]
    proj_up = jnp.concatenate(
        [
            left_grad * left_value * left_gate * (1.0 - left_gate),
            left_grad * left_gate,
            right_grad * right_value * right_gate * (1.0 - right_gate),
            right_grad * right_gate,
        ],
        axis=-1,
    ).astype(jnp.bfloat16)
    gate_up = gate_pre.astype(jnp.bfloat16)
    normed_up = contract("ijh,ch->ijc", proj_up, proj_mat) + contract(
        "ijd,cd->ijc", gate_up, gate_mat
    )
    proj_part = contract("ijc,ijh->ch", normed, proj_up)
    gate_part = contract("ijc,ijd->cd", normed, gate_up)
    return (upstream + norm_back(pair_full, normed_up), proj_part, gate_part)


def reduce_grads(grad_parts):
    return lax.psum((grad_parts[0], grad_parts[1], grad_parts[2]), ("row", "col"))


def local(pair_rep, proj_weight, gate_weight, out_weight, pair_cot):
    rows_here = pair_rep.shape[0]
    full_size = rows_here * lax.axis_size("row")
    pair_full, normed, projected, left_side, right_side, gating = project(
        pair_rep, proj_weight[0], gate_weight[0]
    )
    right_panel = lax.all_gather(right_side, "row", axis=0, tiled=True)
    mix_out = lax.psum_scatter(
        contract("ikc,jkc->ijc", left_side, right_panel).astype(jnp.bfloat16),
        "col",
        scatter_dimension=1,
        tiled=True,
    ).astype(jnp.float32)
    after_out, normed_mix, product = finish(pair_full, mix_out, out_weight[0], gating)
    pair_mid, normed_in, proj_in, left_in, right_in, gating_in = project(
        after_out, proj_weight[1], gate_weight[1]
    )
    left_panel = lax.all_gather(left_in, "col", axis=1, tiled=True)
    columns = left_panel
    mix_in = lax.psum_scatter(
        contract("kic,kjc->ijc", columns, right_in).astype(jnp.bfloat16),
        "row",
        scatter_dimension=0,
        tiled=True,
    ).astype(jnp.float32)
    pair_out, normed_mix_in, product_in = finish(pair_mid, mix_in, out_weight[1], gating_in)
    upstream = pair_cot.astype(jnp.float32)
    grad_in, out_part_in, gate_pre_in = back_head(
        upstream, gating_in, product_in, normed_mix_in, mix_in, out_weight[1]
    )
    grad_cols = lax.all_gather(grad_in, "row", axis=0, tiled=True)
    right_grad_in = contract("kic,ijc->kjc", left_panel, grad_cols)
    left_grad_in = lax.psum_scatter(
        contract("kjc,ijc->kic", right_in, grad_cols).astype(jnp.bfloat16),
        "col",
        scatter_dimension=1,
        tiled=True,
    ).astype(jnp.float32)
    upstream_mid, proj_part_in, gate_part_in = back_tail(
        upstream,
        pair_mid,
        normed_in,
        proj_in,
        left_grad_in,
        right_grad_in,
        gate_pre_in,
        proj_weight[1],
        gate_weight[1],
    )
    summed_in = reduce_grads((proj_part_in, gate_part_in, out_part_in))
    grad_out, out_part_out, gate_pre_out = back_head(
        upstream_mid, gating, product, normed_mix, mix_out, out_weight[0]
    )
    grad_rows = lax.all_gather(grad_out, "col", axis=1, tiled=True)
    left_grad_out = contract("ijc,jkc->ikc", grad_rows, right_panel)
    columns = grad_rows
    right_grad_out = lax.psum_scatter(
        contract("ijc,ikc->jkc", columns, left_side).astype(jnp.bfloat16),
        "row",
        scatter_dimension=0,
        tiled=True,
    ).astype(jnp.float32)
    pair_grad, proj_part_out, gate_part_out = back_tail(
        upstream_mid,
        pair_full,
        normed,
        projected,
        left_grad_out,
        right_grad_out,
        gate_pre_out,
        proj_weight[0],
        gate_weight[0],
    )
    summed_out = reduce_grads((proj_part_out, gate_part_out, out_part_out))
    proj_sum = jnp.stack([summed_out[0], summed_in[0]])
    gate_sum = jnp.stack([summed_out[1], summed_in[1]])
    out_sum = jnp.stack([summed_out[2], summed_in[2]])
    inverse_size = 1.0 / full_size
    return (
        pair_out,
        pair_grad,
        proj_sum * inverse_size,
        gate_sum * inverse_size,
        out_sum * inverse_size,
    )


def solution(mesh):
    in_specs = (P("row", "col", None), P(), P(), P(), P("row", "col", None))
    out_specs = (P("row", "col", None), P("row", "col", None), P(), P(), P())
    return jax.shard_map(local, mesh=mesh, in_specs=in_specs, out_specs=out_specs, check_vma=False)
```

profile of v0, /device:TPU:1, one launch (start us, length us, event | category | flops | bytes accessed | tf_op | source)
XLA Modules:
  0.0 712.1 jit_solution(3298560510583628512)
XLA Ops:
  13.7 56.2 %all-gather.5.cloned.1.call-done = bf16[320,40,128]{2,1,0:T(8,128)(2,1)} async-done(((bf16[20,40,128]{2,1,0:T(8,128)(2,1)}), bf16[320,40,128]{2,1,0:T(8,128)(2,1)}) %all-gather.5.cloned.1.call-update) | async-done | bytes 3276816 | tf_op jit(solution)/shard_map/all_gather | solution.py:94
  69.9 15.3 %copy.74 = bf16[320,40,128]{1,0,2:T(8,128)(2,1)} copy(bf16[320,40,128]{2,1,0:T(8,128)(2,1)} %all-gather.5.cloned.1.call-done) | data formatting | bytes 6553600 | tf_op jit(solution)/shard_map/all_gather | solution.py:94
  85.2 9.5 %convert_bitcast_fusion.3 = bf16[20,320,128]{1,0,2:T(8,128)(2,1)S(1)} fusion(bf16[320,40,128]{1,0,2:T(8,128)(2,1)} %copy.74, bf16[20,40,128]{1,0,2:T(8,128)(2,1)S(1)} %copy.75), kind=kOutput, calls=%fused_computation.3 | convolution fusion | flops 66355200 | bytes 5120000 | tf_op jit(solution)/shard_map/ikc,jkc->ijc/dot_general | solution.py:25
  94.7 3.1 copy.76
  98.0 35.2 %reduce-scatter.7.cloned.1.call-done = bf16[20,40,128]{2,0,1:T(8,128)(2,1)} async-done(((bf16[20,320,128]{2,0,1:T(8,128)(2,1)}), bf16[20,40,128]{2,0,1:T(8,128)(2,1)}) %reduce-scatter.7.cloned.1.call-update) | async-done | bytes 204816 | tf_op jit(solution)/shard_map/reduce_scatter | solution.py:95
  143.6 36.8 %all-gather.7.cloned.1.call-done = bf16[20,320,128]{2,1,0:T(8,128)(2,1)} async-done(((bf16[20,40,128]{2,1,0:T(8,128)(2,1)}), bf16[20,320,128]{2,1,0:T(8,128)(2,1)}) %all-gather.7.cloned.1.call-update) | async-done | bytes 1638416 | tf_op jit(solution)/shard_map/all_gather | solution.py:105
  180.4 3.1 copy.79
  183.5 4.8 convert_bitcast_fusion
  188.3 6.7 copy.80
  195.0 80.4 %reduce-scatter.9.cloned.1.call-done = bf16[20,40,128]{2,1,0:T(8,128)(2,1)} async-done(((bf16[320,40,128]{2,1,0:T(8,128)(2,1)}), bf16[20,40,128]{2,1,0:T(8,128)(2,1)}) %reduce-scatter.9.cloned.1.call-update) | async-done | bytes 204816 | tf_op jit(solution)/shard_map/reduce_scatter | solution.py:107
  283.5 53.2 %all-gather.9.cloned.1.call-done = bf16[320,40,128]{2,1,0:T(8,128)(2,1)} async-done(((bf16[20,40,128]{2,1,0:T(8,128)(2,1)}), bf16[320,40,128]{2,1,0:T(8,128)(2,1)}) %all-gather.9.cloned.1.call-update) | async-done | bytes 3276816 | tf_op jit(solution)/shard_map/all_gather | solution.py:118
  336.7 15.3 %copy.87 = bf16[320,40,128]{1,0,2:T(8,128)(2,1)} copy(bf16[320,40,128]{2,1,0:T(8,128)(2,1)} %all-gather.9.cloned.1.call-done) | data formatting | bytes 6553600 | tf_op jit(solution)/shard_map/all_gather | solution.py:118
  352.0 11.1 %convert_bitcast_fusion.2 = bf16[20,320,128]{1,0,2:T(8,128)(2,1)} fusion(bf16[320,40,128]{1,0,2:T(8,128)(2,1)} %copy.87, bf16[20,40,128]{1,0,2:T(8,128)(2,1)} %copy.78), kind=kOutput, calls=%fused_computation.2 | convolution fusion | flops 66355200 | bytes 5120000 | tf_op jit(solution)/shard_map/kjc,ijc->kic/dot_general | solution.py:25
  363.2 4.6 copy.99
  367.8 3.0 copy.121
  371.1 6.9 fusion.136
  379.9 25.3 %reduce-scatter.13.cloned.1.call-done = bf16[40,2560]{1,0:T(8,128)(2,1)} async-done(((bf16[320,2560]{1,0:T(8,128)(2,1)}), bf16[40,2560]{1,0:T(8,128)(2,1)}) %reduce-scatter.13.cloned.1.call-update) | async-done | bytes 204816
  413.0 38.3 %all-gather.11.cloned.1.call-done = bf16[20,320,128]{2,1,0:T(8,128)(2,1)} async-done(((bf16[20,40,128]{2,1,0:T(8,128)(2,1)}), bf16[20,320,128]{2,1,0:T(8,128)(2,1)}) %all-gather.11.cloned.1.call-update) | async-done | bytes 1638416 | tf_op jit(solution)/shard_map/all_gather | solution.py:141
  451.3 3.1 copy.94
  454.4 3.7 fusion.138
  458.1 6.7 copy.98
  474.2 6.9 fusion.137
  483.1 62.1 %reduce-scatter.11.cloned.1.call-done = bf16[20,40,128]{2,1,0:T(8,128)(2,1)} async-done(((bf16[320,40,128]{2,1,0:T(8,128)(2,1)}), bf16[20,40,128]{2,1,0:T(8,128)(2,1)}) %reduce-scatter.11.cloned.1.call-update) | async-done | bytes 204816 | tf_op jit(solution)/shard_map/reduce_scatter | solution.py:144
  552.7 147.8 %all-reduce.3.cloned.1.call-done = (f32[1,128,512]{2,1,0:T(8,128)}, f32[1,128,512]{2,1,0:T(8,128)}, f32[1,128,128]{2,1,0:T(8,128)}, f32[1,128,128]{2,1,0:T(8,128...) async-done(((f32[1,128,512]{2,1,0:T(8,128)}, f32[1,128,512]{2,1,0:T(8,128)}, f32[1,128,128]{2,1,0:T(8,128)}, f32[1,128,128]{2,1,0:T(8,128)}, f32[1,128,128]{2,1,0:T(8,128)}, ...) | async-done | bytes 786448 | tf_op jit(solution)/shard_map/psum | solution.py:85
  (216 shorter events, 58.2 us)
Async XLA Ops:
  7.2 62.7 %all-gather.5.cloned.1.call-start = ((), (), s32[]{:S(2)}) async-start(), calls=%async_computation.4 | async-start | bytes 3481600 | tf_op jit(solution)/shard_map/all_gather | solution.py:94
  13.2 119.9 %reduce-scatter.7.cloned.1.call-start = ((), (), s32[]{:S(2)}) async-start(), calls=%async_computation.5 | async-start | bytes 2211840 | tf_op jit(solution)/shard_map/reduce_scatter | solution.py:95
  97.8 37.8 %copy-start.58 = (bf16[2,128,128]{2,1,0:T(8,128)(2,1)S(1)}, bf16[2,128,128]{2,1,0:T(8,128)(2,1)}, u32[]{:S(2)}) copy-start(bf16[2,128,128]{2,1,0:T(8,128)(2,1)} %param.8) | copy-start | bytes 196612
  97.8 39.1 %copy-start.5 = (bf16[20,40,128]{2,1,0:T(8,128)(2,1)S(1)}, bf16[20,40,128]{2,1,0:T(8,128)(2,1)}, u32[]{:S(2)}) copy-start(bf16[20,40,128]{2,1,0:T(8,128)(2,1)} %param.5) | copy-start | bytes 614404
  97.9 39.2 %copy-start.30 = (f32[20,40]{1,0:T(8,128)S(1)}, f32[20,40]{1,0:T(8,128)}, u32[]{:S(2)}) copy-start(f32[20,40]{1,0:T(8,128)} %copy-done.29) | copy-start | bytes 9604
  97.9 39.2 %copy-start.50 = (f32[20,40]{1,0:T(8,128)S(1)}, f32[20,40]{1,0:T(8,128)}, u32[]{:S(2)}) copy-start(f32[20,40]{1,0:T(8,128)} %copy-done.49) | copy-start | bytes 9604
  97.9 39.2 %copy-start.68 = (bf16[2,128,128]{2,1,0:T(8,128)(2,1)S(1)}, bf16[2,128,128]{2,1,0:T(8,128)(2,1)}, u32[]{:S(2)}) copy-start(bf16[2,128,128]{2,1,0:T(8,128)(2,1)} %param.7) | copy-start | bytes 196612
  97.9 41.5 %copy-start.35 = (bf16[2,128,512]{2,1,0:T(8,128)(2,1)S(1)}, bf16[2,128,512]{2,1,0:T(8,128)(2,1)}, u32[]{:S(2)}) copy-start(bf16[2,128,512]{2,1,0:T(8,128)(2,1)} %param.6) | copy-start | bytes 786436
  97.9 82.5 %all-gather.7.cloned.1.call-start = ((), (), s32[]{:S(2)}) async-start(), calls=%async_computation.6 | async-start | bytes 1843200 | tf_op jit(solution)/shard_map/all_gather | solution.py:105
  134.3 5.6 copy-start.53
  142.0 133.4 %reduce-scatter.9.cloned.1.call-start = ((), (), s32[]{:S(2)}) async-start(), calls=%async_computation.7 | async-start | bytes 3481600 | tf_op jit(solution)/shard_map/reduce_scatter | solution.py:107
  195.0 141.7 %all-gather.9.cloned.1.call-start = ((), (), s32[]{:S(2)}) async-start(), calls=%async_computation.8 | async-start | bytes 3481600 | tf_op jit(solution)/shard_map/all_gather | solution.py:118
  276.5 5.0 copy-start.4
  276.5 5.0 copy-start.11
  276.6 5.0 copy-start.59
  276.6 5.7 copy-start.33
  283.5 121.6 %reduce-scatter.13.cloned.1.call-start = ((), (), s32[]{:S(2)}) async-start(), calls=%async_computation.11 | async-start | bytes 1843200
  370.8 80.5 %all-gather.11.cloned.1.call-start = ((), (), s32[]{:S(2)}) async-start(), calls=%async_computation.9 | async-start | bytes 1843200 | tf_op jit(solution)/shard_map/all_gather | solution.py:141
  377.9 28.3 %copy-start.3 = (f32[20,40,512]{2,1,0:T(8,128)S(1)}, f32[20,40,512]{2,1,0:T(8,128)}, u32[]{:S(2)}) copy-start(f32[20,40,512]{2,1,0:T(8,128)} %copy-done.2) | copy-start | bytes 4915204
  413.0 132.3 %reduce-scatter.11.cloned.1.call-start = ((), (), s32[]{:S(2)}) async-start(), calls=%async_computation.10 | async-start | bytes 3481600 | tf_op jit(solution)/shard_map/reduce_scatter | solution.py:144
  464.8 235.7 %all-reduce.3.cloned.1.call-start = ((), (), s32[]{:S(2)}) async-start(), calls=%async_computation.12 | async-start | bytes 1572864 | tf_op jit(solution)/shard_map/psum | solution.py:85
  466.9 4.9 copy-start.6
  481.1 64.1 %copy-start.1 = (f32[20,40,512]{2,1,0:T(8,128)S(1)}, f32[20,40,512]{2,1,0:T(8,128)}, u32[]{:S(2)}) copy-start(f32[20,40,512]{2,1,0:T(8,128)} %copy-done) | copy-start | bytes 4915204
  483.1 64.1 %copy-start.52 = (f32[20,40]{1,0:T(8,128)S(1)}, f32[20,40]{1,0:T(8,128)}, u32[]{:S(2)}) copy-start(f32[20,40]{1,0:T(8,128)} %copy-done.49) | copy-start | bytes 9604
  (56 other events, 129.2 us)
Sparse Core Ops, SparseCore 0:
  13.3 56.4 all-gather.4
  98.0 35.1 reduce-scatter.6
  142.1 38.2 all-gather.6
  195.1 80.2 reduce-scatter.8
  283.6 53.0 all-gather.8
  370.9 34.1 reduce-scatter.12
  413.1 38.1 all-gather.10
  465.0 80.2 reduce-scatter.10
  552.3 148.2 all-reduce.2
where the time goes:
time: 713 us; the launch traced here: 712 us
  waiting for transfers between devices  535 us (75%)
  local copies, waits for them, and re-layouts  74.5 us (10%)
  matrix products  65 us (9%)
  other arithmetic  21.3 us (3%)
  between operations  14.8 us (2%)
    psum x1, waiting for transfers between devices, reduce_grads(): lax.psum((grad_parts[0], grad_parts[1], grad_parts[2]), ('row', 'col'))  148 us
    reduce_scatter x1, waiting for transfers between devices, local(): lax.psum_scatter(contract('kic,kjc->ijc', columns, right_in).astype(jnp.b...  80.4 us
    dot_general x24, matrix products, contract(): jnp.einsum(pattern, first_op, second_op, preferred_element_type=jnp.float32)  65 us
    reduce_scatter x1, waiting for transfers between devices, local(): lax.psum_scatter(contract('ijc,ikc->jkc', columns, left_side).astype(jnp....  62.1 us
    all_gather x1, waiting for transfers between devices, local(): right_panel = lax.all_gather(right_side, 'row', axis=0, tiled=True)  56.2 us
    all_gather x1, waiting for transfers between devices, local(): grad_cols = lax.all_gather(grad_in, 'row', axis=0, tiled=True)  53.2 us
    all_gather x1, waiting for transfers between devices, local(): grad_rows = lax.all_gather(grad_out, 'col', axis=1, tiled=True)  38.3 us
    all_gather x1, waiting for transfers between devices, local(): left_panel = lax.all_gather(left_in, 'col', axis=1, tiled=True)  36.8 us
  transfers between devices with their start and end apart: 9, of which 9 were waited for; matrix products, arithmetic and copies ran while one was open for 4% of the time, Pallas kernels for 0%

commit v1 on v0

v1 whole, which is shorter than its diff:
```python
import functools

import jax
import jax.numpy as jnp
from jax import lax
from jax.experimental import pallas as pl
from jax.experimental.pallas import tpu as pltpu
from jax.sharding import PartitionSpec as P

EPSILON = 1e-05
F32 = jnp.float32
BF16 = jnp.bfloat16
AXES = ("row", "col")

PARTS_R, PARTS_C = 16, 8
ROWS, COLS, CHANNELS = 20, 40, 128
PER = 3
TILES = 7
SUBS = 8
LANES = 128
SIZE = 320
WIDE = 384


def dot(first_op, second_op, first_dim, second_dim):
    return lax.dot_general(
        first_op,
        second_op,
        (((first_dim,), (second_dim,)), ((), ())),
        preferred_element_type=F32,
    )


def mean0(values):
    return jnp.sum(values, axis=0, keepdims=True) * (1.0 / CHANNELS)


def norm_parts(values):
    centered = values - mean0(values)
    inverse = lax.rsqrt(mean0(centered * centered) + EPSILON)
    return centered * inverse, inverse


def norm_back(normed, inverse, upstream):
    return inverse * (upstream - mean0(upstream) - normed * mean0(upstream * normed))


def block_in(ref):
    values = ref[...].astype(F32)
    tiles = []
    for s in range(TILES):
        low = s * PER * COLS
        high = min(low + PER * COLS, ROWS * COLS)
        piece = values[low:high]
        piece = jnp.concatenate([piece, jnp.zeros((LANES - (high - low), CHANNELS), F32)], axis=0)
        tiles.append(piece.T)
    return jnp.concatenate(tiles, axis=1)


def block_out(values):
    pieces = []
    for s in range(TILES):
        count = min(PER * COLS, ROWS * COLS - s * PER * COLS)
        pieces.append(values[:, s * LANES : (s + 1) * LANES].T[:count])
    return jnp.concatenate(pieces, axis=0)


def pack(parts, out_ref, wide):
    stride = SUBS * len(parts)
    for a, part in enumerate(parts):
        for s in range(TILES):
            wide[pl.ds(a * SUBS + s, CHANNELS, stride=stride), :] = part[:, s * LANES : (s + 1) * LANES]
        wide[pl.ds(a * SUBS + TILES, CHANNELS, stride=stride), :] = jnp.zeros((CHANNELS, LANES), F32)
    out_ref[...] = wide[...].astype(BF16)


def unpack(ref, wide, count):
    wide[...] = ref[...].astype(F32)
    stride = SUBS * count
    return [
        jnp.concatenate(
            [wide[pl.ds(a * SUBS + s, CHANNELS, stride=stride), :] for s in range(TILES)], axis=1
        )
        for a in range(count)
    ]


def lanes_of(shape):
    return lax.broadcasted_iota(jnp.int32, shape, 1)


def matrix_in(ref, a):
    lane = lanes_of((LANES, LANES))
    pieces = [
        ref[:, c].astype(F32)[:, a * SUBS : (a + 1) * SUBS].reshape(LANES, LANES)
        for c in range(PARTS_C)
    ]
    rows = []
    for t in range(PER):
        turned = [
            pltpu.roll(pieces[c], ((c - t) * COLS) % LANES, 1) if (c - t) * COLS % LANES else pieces[c]
            for c in range(PARTS_C)
        ]
        tiles = []
        for q in range(WIDE // LANES):
            tile = jnp.zeros((LANES, LANES), F32)
            for c in range(PARTS_C):
                low, high = c * COLS - q * LANES, (c + 1) * COLS - q * LANES
                if high <= 0 or low >= LANES:
                    continue
                tile = jnp.where((lane >= low) & (lane < high), turned[c], tile)
            tiles.append(tile)
        rows.append(jnp.concatenate(tiles, axis=1))
    return jnp.concatenate(rows, axis=0).astype(BF16)


def matrix_out(values, a, wide):
    lane = lanes_of((LANES, LANES))
    for c in range(PARTS_C):
        low = c * COLS
        first, last = low // LANES, (low + COLS - 1) // LANES
        piece = jnp.zeros((LANES, LANES), F32)
        for t in range(PER):
            band = values[t * LANES : (t + 1) * LANES]
            source = band[:, first * LANES : (first + 1) * LANES]
            if last != first:
                source = jnp.where(lane >= low % LANES, source, band[:, last * LANES : (last + 1) * LANES])
            shift = ((t - c) * COLS) % LANES
            if shift:
                source = pltpu.roll(source, shift, 1)
            piece = jnp.where((lane >= t * COLS) & (lane < (t + 1) * COLS), source, piece)
        wide[:, c, a * SUBS : (a + 1) * SUBS, :] = piece.reshape(PARTS_R, SUBS, LANES)


def residue_of(index):
    part, s, t = (index % LANES) // SUBS, index % SUBS, index // LANES
    inner = PER * s + t
    return jnp.where(inner < ROWS, part * ROWS + inner, -1)


def first_to_second():
    first = lax.broadcasted_iota(jnp.int32, (WIDE, WIDE), 1)
    second = lax.broadcasted_iota(jnp.int32, (WIDE, WIDE), 0)
    return jnp.where(residue_of(first) == second, 1.0, 0.0).astype(BF16)


def second_to_first():
    first = lax.broadcasted_iota(jnp.int32, (WIDE, WIDE), 0)
    second = lax.broadcasted_iota(jnp.int32, (WIDE, WIDE), 1)
    return jnp.where(residue_of(first) == second, 1.0, 0.0).astype(BF16)


def project(normed, proj_mat):
    projected = dot(proj_mat, normed, 0, 0)
    return [projected[q * CHANNELS : (q + 1) * CHANNELS] for q in range(4)]


def edges(normed, proj_mat):
    p1, p2, p3, p4 = project(normed, proj_mat)
    return jax.nn.sigmoid(p1) * p2, jax.nn.sigmoid(p3) * p4


def gate_of(normed, gate_mat):
    return jax.nn.sigmoid(dot(gate_mat, normed, 0, 0))


def back_head(upstream, gating, product, normed_mix, mix_normed, mix_inverse, out_mat):
    through = (upstream * gating).astype(BF16)
    gate_up = (upstream * product * gating * (1.0 - gating)).astype(BF16)
    mix_up = dot(out_mat, through, 1, 0)
    out_part = dot(normed_mix, through, 1, 1)
    return norm_back(mix_normed, mix_inverse, mix_up), out_part, gate_up


def back_tail(upstream, pair_full, normed, left_grad, right_grad, gate_up, proj_mat, gate_mat):
    p1, p2, p3, p4 = project(normed, proj_mat)
    s1, s3 = jax.nn.sigmoid(p1), jax.nn.sigmoid(p3)
    proj_up = jnp.concatenate(
        [
            left_grad * p2 * s1 * (1.0 - s1),
            left_grad * s1,
            right_grad * p4 * s3 * (1.0 - s3),
            right_grad * s3,
        ],
        axis=0,
    ).astype(BF16)
    normed_up = dot(proj_mat, proj_up, 1, 0) + dot(gate_mat, gate_up, 1, 0)
    proj_part = dot(normed, proj_up, 1, 1)
    gate_part = dot(normed, gate_up, 1, 1)
    pair_normed, pair_inverse = norm_parts(pair_full)
    return upstream + norm_back(pair_normed, pair_inverse, normed_up), proj_part, gate_part


def start_kernel(pair_ref, proj_ref, gate_ref, message_ref, normed_ref, gating_ref, wide):
    normed = norm_parts(block_in(pair_ref))[0].astype(BF16)
    normed_ref[...] = normed
    pack(edges(normed, proj_ref[0]), message_ref, wide)
    gating_ref[...] = gate_of(normed, gate_ref[0])


def middle_kernel(
    mix_ref, pair_ref, gating0_ref, proj_ref, gate_ref, out_ref, message_ref, normed_ref, gating_ref, after_ref,
    narrow, wide,
):
    (mix,) = unpack(mix_ref, narrow, 1)
    normed_mix = norm_parts(mix)[0].astype(BF16)
    product = dot(out_ref[0], normed_mix, 0, 0)
    after = (block_in(pair_ref) + gating0_ref[...] * product).astype(BF16)
    after_ref[...] = after
    normed = norm_parts(after.astype(F32))[0].astype(BF16)
    normed_ref[...] = normed
    pack(edges(normed, proj_ref[1]), message_ref, wide)
    gating_ref[...] = gate_of(normed, gate_ref[1])


def turn_kernel(
    mix_ref, after_ref, gating_ref, cot_ref, out_ref, pair_out_ref, message_ref, gate_up_ref, out_part_ref, narrow
):
    (mix,) = unpack(mix_ref, narrow, 1)
    mix_normed, mix_inverse = norm_parts(mix)
    normed_mix = mix_normed.astype(BF16)
    product = dot(out_ref[1], normed_mix, 0, 0)
    gating = gating_ref[...]
    pair_out_ref[...] = block_out(after_ref[...].astype(F32) + gating * product).astype(BF16)
    mix_grad, out_part, gate_up = back_head(
        block_in(cot_ref), gating, product, normed_mix, mix_normed, mix_inverse, out_ref[1]
    )
    out_part_ref[...] = out_part
    gate_up_ref[...] = gate_up
    pack([mix_grad], message_ref, narrow)


def back_kernel(
    grads_ref, cot_ref, after_ref, normed1_ref, gate_up1_ref, mix_ref, gating0_ref, proj_ref, gate_ref, out_ref,
    message_ref, upstream_ref, gate_up_ref, proj_part_ref, gate_part_ref, out_part_ref, narrow, wide,
):
    left_grad, right_grad = unpack(grads_ref, wide, 2)
    upstream, proj_part, gate_part = back_tail(
        block_in(cot_ref), after_ref[...].astype(F32), normed1_ref[...], left_grad, right_grad, gate_up1_ref[...],
        proj_ref[1], gate_ref[1],
    )
    proj_part_ref[...] = proj_part
    gate_part_ref[...] = gate_part
    upstream_ref[...] = upstream
    (mix,) = unpack(mix_ref, narrow, 1)
    mix_normed, mix_inverse = norm_parts(mix)
    normed_mix = mix_normed.astype(BF16)
    product = dot(out_ref[0], normed_mix, 0, 0)
    mix_grad, out_part, gate_up = back_head(
        upstream, gating0_ref[...], product, normed_mix, mix_normed, mix_inverse, out_ref[0]
    )
    out_part_ref[...] = out_part
    gate_up_ref[...] = gate_up
    pack([mix_grad], message_ref, narrow)


def last_kernel(
    grads_ref, upstream_ref, pair_ref, normed_ref, gate_up_ref, proj_ref, gate_ref, proj1_ref, gate1_ref, out1_ref,
    out0_ref, pair_grad_ref, message_ref, wide,
):
    left_grad, right_grad = unpack(grads_ref, wide, 2)
    pair_grad, proj_part, gate_part = back_tail(
        upstream_ref[...], block_in(pair_ref), normed_ref[...], left_grad, right_grad, gate_up_ref[...],
        proj_ref[0], gate_ref[0],
    )
    pair_grad_ref[...] = block_out(pair_grad)
    parts = [proj_part[:, q * LANES : (q + 1) * LANES] for q in range(4)]
    parts += [proj1_ref[:, q * LANES : (q + 1) * LANES] for q in range(4)]
    parts += [gate_part, gate1_ref[...], out0_ref[...], out1_ref[...]]
    for q in range(2 * SUBS):
        wide[pl.ds(q, CHANNELS, stride=2 * SUBS), :] = parts[q] if q < len(parts) else jnp.zeros((CHANNELS, LANES), F32)
    message_ref[...] = wide[...].astype(BF16)


def sum_kernel(parts_ref, total_ref):
    total = jnp.sum(parts_ref[...].astype(F32), axis=0, keepdims=True) * (1.0 / SIZE)
    total_ref[...] = jnp.broadcast_to(total, total_ref.shape).astype(BF16)


def spread_kernel(sums_ref, proj_ref, gate_ref, out_ref, wide):
    wide[...] = sums_ref[...].astype(F32)
    rows = [wide[pl.ds(q, CHANNELS, stride=2 * SUBS), :] for q in range(12)]
    for l in range(2):
        proj_ref[l] = jnp.concatenate(rows[4 * l : 4 * l + 4], axis=1)
        gate_ref[l] = rows[8 + l]
        out_ref[l] = rows[10 + l]


def outgoing_kernel(edges_ref, mix_ref, left_ref, right_ref, wide):
    left, right = matrix_in(edges_ref, 0), matrix_in(edges_ref, 1)
    right = dot(first_to_second(), right, 1, 0).astype(BF16)
    left_ref[...], right_ref[...] = left, right
    matrix_out(dot(left, right, 1, 1), 0, wide)
    mix_ref[...] = wide[...].astype(BF16)


def incoming_kernel(edges_ref, mix_ref, left_ref, right_ref, wide):
    left, right = matrix_in(edges_ref, 0), matrix_in(edges_ref, 1)
    left_ref[...], right_ref[...] = left, right
    turned = dot(second_to_first(), left, 1, 1).astype(BF16)
    matrix_out(dot(turned, right, 1, 0), 0, wide)
    mix_ref[...] = wide[...].astype(BF16)


def incoming_back_kernel(grad_ref, left_ref, right_ref, grads_ref, wide):
    grad = dot(first_to_second(), matrix_in(grad_ref, 0), 1, 0).astype(BF16)
    matrix_out(dot(right_ref[...], grad, 1, 1), 0, wide)
    matrix_out(dot(left_ref[...], grad, 1, 0), 1, wide)
    grads_ref[...] = wide[...].astype(BF16)


def outgoing_back_kernel(grad_ref, left_ref, right_ref, grads_ref, wide):
    grad = matrix_in(grad_ref, 0)
    matrix_out(dot(grad, right_ref[...], 1, 0), 0, wide)
    turned = dot(second_to_first(), grad, 1, 1).astype(BF16)
    matrix_out(dot(turned, left_ref[...], 1, 0), 1, wide)
    grads_ref[...] = wide[...].astype(BF16)


def call(kernel, name, outs, scratch, *operands):
    return pl.pallas_call(
        kernel,
        out_shape=[jax.ShapeDtypeStruct(shape, kind) for shape, kind in outs],
        scratch_shapes=[pltpu.VMEM(shape, F32) for shape in scratch],
        compiler_params=pltpu.CompilerParams(vmem_limit_bytes=48 * 1024 * 1024),
        name=name,
    )(*operands)


def exchange(message):
    rows = message.size // (PARTS_R * PARTS_C * LANES)
    message = message.reshape(PARTS_R * PARTS_C, rows, LANES)
    return lax.all_to_all(message, AXES, 0, 0, tiled=True)


ONE = (CHANNELS * SUBS, LANES)
TWO = (CHANNELS * SUBS * 2, LANES)
MATRIX_ONE = (PARTS_R, PARTS_C, SUBS, LANES)
MATRIX_TWO = (PARTS_R, PARTS_C, SUBS * 2, LANES)
FLAT = (CHANNELS, TILES * LANES)
SQUARE = (WIDE, WIDE)


def local(pair_rep, proj_weight, gate_weight, out_weight, pair_cot):
    pair = pair_rep.reshape(ROWS * COLS, CHANNELS)
    cot = pair_cot.reshape(ROWS * COLS, CHANNELS)
    edges0, normed0, gating0 = call(
        start_kernel, "start", [(TWO, BF16), (FLAT, BF16), (FLAT, F32)], [TWO], pair, proj_weight, gate_weight
    )
    mix0, left0, right0 = call(
        outgoing_kernel, "outgoing", [(MATRIX_ONE, BF16), (SQUARE, BF16), (SQUARE, BF16)], [MATRIX_ONE],
        exchange(edges0).reshape(MATRIX_TWO),
    )
    mix0 = exchange(mix0).reshape(ONE)
    edges1, normed1, gating1, after = call(
        middle_kernel, "middle", [(TWO, BF16), (FLAT, BF16), (FLAT, F32), (FLAT, BF16)], [ONE, TWO],
        mix0, pair, gating0, proj_weight, gate_weight, out_weight,
    )
    mix1, left1, right1 = call(
        incoming_kernel, "incoming", [(MATRIX_ONE, BF16), (SQUARE, BF16), (SQUARE, BF16)], [MATRIX_ONE],
        exchange(edges1).reshape(MATRIX_TWO),
    )
    mix1 = exchange(mix1).reshape(ONE)
    pair_out, grad1, gate_up1, out_part1 = call(
        turn_kernel, "turn", [((ROWS * COLS, CHANNELS), BF16), (ONE, BF16), (FLAT, BF16), ((CHANNELS, CHANNELS), F32)],
        [ONE], mix1, after, gating1, cot, out_weight,
    )
    (grads1,) = call(
        incoming_back_kernel, "incoming_back", [(MATRIX_TWO, BF16)], [MATRIX_TWO],
        exchange(grad1).reshape(MATRIX_ONE), left1, right1,
    )
    grads1 = exchange(grads1).reshape(TWO)
    grad0, upstream, gate_up0, proj_part1, gate_part1, out_part0 = call(
        back_kernel, "back",
        [
            (ONE, BF16), (FLAT, F32), (FLAT, BF16), ((CHANNELS, 4 * CHANNELS), F32), ((CHANNELS, CHANNELS), F32),
            ((CHANNELS, CHANNELS), F32),
        ],
        [ONE, TWO], grads1, cot, after, normed1, gate_up1, mix0, gating0, proj_weight, gate_weight, out_weight,
    )
    (grads0,) = call(
        outgoing_back_kernel, "outgoing_back", [(MATRIX_TWO, BF16)], [MATRIX_TWO],
        exchange(grad0).reshape(MATRIX_ONE), left0, right0,
    )
    grads0 = exchange(grads0).reshape(TWO)
    pair_grad, parts = call(
        last_kernel, "last", [((ROWS * COLS, CHANNELS), F32), (TWO, BF16)], [TWO],
        grads0, upstream, pair, normed0, gate_up0, proj_weight, gate_weight, proj_part1, gate_part1, out_part1,
        out_part0,
    )
    (sums,) = call(sum_kernel, "sum", [((CHANNELS, 2 * SUBS, LANES), BF16)], [], exchange(parts))
    proj_grad, gate_grad, out_grad = call(
        spread_kernel, "spread",
        [((2, CHANNELS, 4 * CHANNELS), F32), ((2, CHANNELS, CHANNELS), F32), ((2, CHANNELS, CHANNELS), F32)],
        [TWO], exchange(sums).reshape(TWO),
    )
    return (
        pair_out.reshape(ROWS, COLS, CHANNELS),
        pair_grad.reshape(ROWS, COLS, CHANNELS),
        proj_grad,
        gate_grad,
        out_grad,
    )


def solution(mesh):
    in_specs = (P("row", "col", None), P(), P(), P(), P("row", "col", None))
    out_specs = (P("row", "col", None), P("row", "col", None), P(), P(), P())
    return jax.shard_map(local, mesh=mesh, in_specs=in_specs, out_specs=out_specs, check_vma=False)
```

time: 713 us -> 190 us (0.27)
  waiting for transfers between devices: 535 us -> 0 us
  blocking collectives: 0 us -> 173 us
  local copies, waits for them, and re-layouts: 74.5 us -> 2.74 us
  matrix products: 65 us -> 0 us
  other arithmetic: 21.3 us -> 0 us
  between operations: 14.8 us -> 0.74 us
  Pallas kernels: 0 us -> 13.6 us
    all_gather x4 -> x0, waiting for transfers between devices: 184 us -> none  [the longest x1 56.2 us: local(): right_panel = lax.all_gather(right_side, 'row', axis=0, tiled=True)]
    reduce_scatter x3 -> x0, waiting for transfers between devices: 178 us -> none  [the longest x1 80.4 us: local(): lax.psum_scatter(contract('kic,kjc->ijc', columns, right_in).astype(jnp.b...]
    all_to_all x0 -> x10, blocking collectives: none -> 173 us  [exchange(): return lax.all_to_all(message, AXES, 0, 0, tiled=True)]
    psum x1 -> x0, waiting for transfers between devices: 148 us -> none  [reduce_grads(): lax.psum((grad_parts[0], grad_parts[1], grad_parts[2]), ('row', 'col'))]
    dot_general x24 -> x0, matrix products: 65 us -> none  [contract(): jnp.einsum(pattern, first_op, second_op, preferred_element_type=jnp.float32)]
    all_gather x4 -> x0, local copies, waits for them, and re-layouts: 36.9 us -> none  [the longest x1 15.3 us: local(): right_panel = lax.all_gather(right_side, 'row', axis=0, tiled=True)]
    unnamed x10 -> x0, waiting for transfers between devices: 25.4 us -> none
    pallas_call x0 -> x11, Pallas kernels: none -> 13.6 us  [call(): pl.pallas_call(kernel, out_shape=[jax.ShapeDtypeStruct(shape, kind) for s...]
  transfers between devices with their start and end apart: 9 -> 0, of which waited for: 9 -> 0; matrix products, arithmetic and copies ran while one was open for 4% -> 0% of each run, Pallas kernels for 0% -> 0%
where the time goes in v1:
time: 190 us
  blocking collectives  173 us (91%)
  Pallas kernels  13.6 us (7%)
  local copies, waits for them, and re-layouts  2.74 us (1%)
    all_to_all x10, blocking collectives, exchange(): return lax.all_to_all(message, AXES, 0, 0, tiled=True)  173 us
    pallas_call x11, Pallas kernels, call(): pl.pallas_call(kernel, out_shape=[jax.ShapeDtypeStruct(shape, kind) for s...  13.6 us

profile of v1, /device:TPU:1, one launch (start us, length us, event | category | flops | bytes accessed | tf_op | source)
XLA Modules:
  0.0 189.7 jit_solution(6468522381674934738)
XLA Ops:
  0.6 0.9 copy-done
  1.6 0.9 copy-done.2
  2.5 0.8 copy-done.4
  3.4 0.9 start.1
  4.2 24.2 %all_to_all.50 = bf16[128,16,128]{2,1,0:T(8,128)(2,1)S(1)} all-to-all(bf16[128,16,128]{2,1,0:T(8,128)(2,1)S(1)} %bitcast.41), channel_id=1, replica_groups=mesh['row'=16,'col'=8] {'row','col'}, dimensions={0} | all-to-all | bytes 1048576 | tf_op jit(solution)/shard_map/all_to_all | solution.py:333
  28.4 1.2 outgoing.1
  29.6 15.7 %all_to_all.51 = bf16[128,8,128]{2,1,0:T(8,128)(2,1)S(1)} all-to-all(bf16[128,8,128]{2,1,0:T(8,128)(2,1)S(1)} %bitcast.44), channel_id=1, replica_groups=mesh['row'=16,'col'=8] {'row','col'}, dimensions={0} | all-to-all | bytes 524288 | tf_op jit(solution)/shard_map/all_to_all | solution.py:333
  45.3 1.1 middle.1
  46.5 17.0 %all_to_all.52 = bf16[128,16,128]{2,1,0:T(8,128)(2,1)S(1)} all-to-all(bf16[128,16,128]{2,1,0:T(8,128)(2,1)S(1)} %bitcast.40), channel_id=1, replica_groups=mesh['row'=16,'col'=8] {'row','col'}, dimensions={0} | all-to-all | bytes 1048576 | tf_op jit(solution)/shard_map/all_to_all | solution.py:333
  63.5 1.1 incoming.1
  64.6 15.7 %all_to_all.53 = bf16[128,8,128]{2,1,0:T(8,128)(2,1)S(1)} all-to-all(bf16[128,8,128]{2,1,0:T(8,128)(2,1)S(1)} %bitcast.45), channel_id=1, replica_groups=mesh['row'=16,'col'=8] {'row','col'}, dimensions={0} | all-to-all | bytes 524288 | tf_op jit(solution)/shard_map/all_to_all | solution.py:333
  80.3 1.4 turn.1
  81.7 15.1 %all_to_all.54 = bf16[128,8,128]{2,1,0:T(8,128)(2,1)S(1)} all-to-all(bf16[128,8,128]{2,1,0:T(8,128)(2,1)S(1)} %bitcast.43), channel_id=1, replica_groups=mesh['row'=16,'col'=8] {'row','col'}, dimensions={0} | all-to-all | bytes 524288 | tf_op jit(solution)/shard_map/all_to_all | solution.py:333
  96.8 1.3 incoming_back.1
  98.0 17.0 %all_to_all.55 = bf16[128,16,128]{2,1,0:T(8,128)(2,1)S(1)} all-to-all(bf16[128,16,128]{2,1,0:T(8,128)(2,1)S(1)} %bitcast.29), channel_id=1, replica_groups=mesh['row'=16,'col'=8] {'row','col'}, dimensions={0} | all-to-all | bytes 1048576 | tf_op jit(solution)/shard_map/all_to_all | solution.py:333
  115.1 1.8 back.1
  116.9 15.7 %all_to_all.56 = bf16[128,8,128]{2,1,0:T(8,128)(2,1)S(1)} all-to-all(bf16[128,8,128]{2,1,0:T(8,128)(2,1)S(1)} %bitcast.42), channel_id=1, replica_groups=mesh['row'=16,'col'=8] {'row','col'}, dimensions={0} | all-to-all | bytes 524288 | tf_op jit(solution)/shard_map/all_to_all | solution.py:333
  132.6 1.2 outgoing_back.1
  133.8 17.0 %all_to_all.57 = bf16[128,16,128]{2,1,0:T(8,128)(2,1)S(1)} all-to-all(bf16[128,16,128]{2,1,0:T(8,128)(2,1)S(1)} %bitcast.30), channel_id=1, replica_groups=mesh['row'=16,'col'=8] {'row','col'}, dimensions={0} | all-to-all | bytes 1048576 | tf_op jit(solution)/shard_map/all_to_all | solution.py:333
  150.8 2.3 %last.1 = (f32[800,128]{1,0:T(8,128)}, bf16[2048,128]{1,0:T(8,128)(2,1)S(1)}) custom-call(bf16[2048,128]{1,0:T(8,128)(2,1)S(1)} %bitcast.25, f32[128,896]{1,0:T(8,128)S(1)} %get-tuple-element.49.upstream_ref, bf16[800,128]{1,0:T(8,128)(2,1)S(1)} %bitcast.33, bf16[128,896]{1,0:T(8,128)(2,1)S(1)} %get-tuple-element.50.normed_ref, ...), custom_call_target="tpu_custom_call" | custom-call | tf_op jit(solution)/shard_map/last/pallas_call | solution.py:321
  153.2 17.6 %all_to_all.58.parts_ref = bf16[128,16,128]{2,1,0:T(8,128)(2,1)S(1)} all-to-all(bf16[128,16,128]{2,1,0:T(8,128)(2,1)S(1)} %bitcast.39), channel_id=1, replica_groups=mesh['row'=16,'col'=8] {'row','col'}, dimensions={0} | all-to-all | bytes 1048576 | tf_op jit(solution)/shard_map/all_to_all | solution.py:333
  170.8 0.2 sum.1
  170.9 17.6 %all_to_all.59 = bf16[128,16,128]{2,1,0:T(8,128)(2,1)S(1)} all-to-all(bf16[128,16,128]{2,1,0:T(8,128)(2,1)S(1)} %sum.1), channel_id=1, replica_groups=mesh['row'=16,'col'=8] {'row','col'}, dimensions={0} | all-to-all | bytes 1048576 | tf_op jit(solution)/shard_map/all_to_all | solution.py:333
  188.6 1.1 spread.1
  (13 shorter events, 0.0 us)
Async XLA Ops:
  0.6 1.0 copy-start
  1.6 0.9 copy-start.2
  2.5 0.8 copy-start.4
  28.4 16.9 %copy-start.5 = (bf16[2,128,128]{2,1,0:T(8,128)(2,1)S(1)}, bf16[2,128,128]{2,1,0:T(8,128)(2,1)}, u32[]{:S(2)}) copy-start(bf16[2,128,128]{2,1,0:T(8,128)(2,1)} %gate_ref.7) | copy-start | bytes 196612
  28.4 16.9 %copy-start.7 = (bf16[2,128,128]{2,1,0:T(8,128)(2,1)S(1)}, bf16[2,128,128]{2,1,0:T(8,128)(2,1)}, u32[]{:S(2)}) copy-start(bf16[2,128,128]{2,1,0:T(8,128)(2,1)} %out_ref.5) | copy-start | bytes 196612
  29.6 15.7 %copy-start.1 = (bf16[2,128,512]{2,1,0:T(8,128)(2,1)S(1)}, bf16[2,128,512]{2,1,0:T(8,128)(2,1)}, u32[]{:S(2)}) copy-start(bf16[2,128,512]{2,1,0:T(8,128)(2,1)} %proj_ref.7) | copy-start | bytes 786436
  29.6 15.7 %copy-start.3 = (bf16[20,40,128]{2,1,0:T(8,128)(2,1)S(1)}, bf16[20,40,128]{2,1,0:T(8,128)(2,1)}, u32[]{:S(2)}) copy-start(bf16[20,40,128]{2,1,0:T(8,128)(2,1)} %param.5) | copy-start | bytes 614404
  64.6 15.7 %copy-start.6 = (bf16[20,40,128]{2,1,0:T(8,128)(2,1)S(1)}, bf16[20,40,128]{2,1,0:T(8,128)(2,1)}, u32[]{:S(2)}) copy-start(bf16[20,40,128]{2,1,0:T(8,128)(2,1)} %param.9) | copy-start | bytes 614404

commit v2 on v1

v2 whole, which is shorter than its diff:
```python
import jax
import jax.numpy as jnp
from jax import lax
from jax.experimental import pallas as pl
from jax.experimental.pallas import tpu as pltpu
from jax.sharding import PartitionSpec as P

EPSILON = 1e-05
F32 = jnp.float32
BF16 = jnp.bfloat16
AXES = ("row", "col")

PARTS_R, PARTS_C = 16, 8
DEVICES = PARTS_R * PARTS_C
ROWS, COLS, CHANNELS = 20, 40, 128
PER = 3
TILES = 7
SUBS = 8
LANES = 128
SIZE = 320
WIDE = 384
SINGLE, DOUBLE, WEIGHTS = 8, 14, 12


def dot(first_op, second_op, first_dim, second_dim):
    return lax.dot_general(
        first_op,
        second_op,
        (((first_dim,), (second_dim,)), ((), ())),
        preferred_element_type=F32,
    )


def mean0(values):
    return jnp.sum(values, axis=0, keepdims=True) * (1.0 / CHANNELS)


def norm_parts(values):
    centered = values - mean0(values)
    inverse = lax.rsqrt(mean0(centered * centered) + EPSILON)
    return centered * inverse, inverse


def norm_back(normed, inverse, upstream):
    return inverse * (upstream - mean0(upstream) - normed * mean0(upstream * normed))


def sigmoid(values):
    return 0.5 * jnp.tanh(0.5 * values) + 0.5


def block_in(ref):
    values = ref[...].astype(F32)
    tiles = []
    for s in range(TILES):
        low = s * PER * COLS
        high = min(low + PER * COLS, ROWS * COLS)
        piece = values[low:high]
        piece = jnp.concatenate([piece, jnp.zeros((LANES - (high - low), CHANNELS), F32)], axis=0)
        tiles.append(piece.T)
    return jnp.concatenate(tiles, axis=1)


def block_out(values):
    pieces = []
    for s in range(TILES):
        count = min(PER * COLS, ROWS * COLS - s * PER * COLS)
        pieces.append(values[:, s * LANES : (s + 1) * LANES].T[:count])
    return jnp.concatenate(pieces, axis=0)


def rows_of(parts):
    return SINGLE if parts == 1 else DOUBLE


def pitch_of(parts):
    return SINGLE + 1 if parts == 1 else DOUBLE


def pack(parts, out_ref, wide):
    pitch = pitch_of(len(parts))
    for a, part in enumerate(parts):
        for s in range(TILES):
            wide[pl.ds(a * TILES + s, CHANNELS, stride=pitch), :] = part[:, s * LANES : (s + 1) * LANES]
    if len(parts) == 1:
        wide[pl.ds(TILES, CHANNELS, stride=pitch), :] = jnp.zeros((CHANNELS, LANES), F32)
        for d in range(0, CHANNELS, 2):
            two = [wide[e * pitch : e * pitch + SINGLE, :] for e in (d, d + 1)]
            out_ref[d * SINGLE : (d + 2) * SINGLE, :] = jnp.concatenate(two, axis=0).astype(BF16)
    else:
        out_ref[...] = wide[...].astype(BF16)


def unpack(ref, wide, count):
    pitch = pitch_of(count)
    if count == 1:
        for d in range(0, CHANNELS, 2):
            two = ref[d * SINGLE : (d + 2) * SINGLE, :].astype(F32)
            for e in range(2):
                wide[(d + e) * pitch : (d + e) * pitch + SINGLE, :] = two[e * SINGLE : (e + 1) * SINGLE]
    else:
        wide[...] = ref[...].astype(F32)
    return [
        jnp.concatenate([wide[pl.ds(a * TILES + s, CHANNELS, stride=pitch), :] for s in range(TILES)], axis=1)
        for a in range(count)
    ]


def matrix_in(wide, a, count):
    lane = lax.broadcasted_iota(jnp.int32, (LANES, LANES), 1)
    real = lax.broadcasted_iota(jnp.int32, (LANES, LANES), 0) % SUBS < TILES
    stride = rows_of(count)
    pieces = []
    for c in range(PARTS_C):
        starts = [(r * PARTS_C + c) * stride + a * TILES for r in range(PARTS_R)]
        piece = jnp.concatenate([wide[start : start + SUBS, :] for start in starts], axis=0)
        pieces.append((piece if count == 1 else jnp.where(real, piece, 0.0)).astype(BF16))
    rows = []
    for t in range(PER):
        turned = [
            pltpu.roll(pieces[c], ((c - t) * COLS) % LANES, 1) if (c - t) * COLS % LANES else pieces[c]
            for c in range(PARTS_C)
        ]
        tiles = []
        for q in range(WIDE // LANES):
            low, high = q * LANES, (q + 1) * LANES
            inside = [c for c in range(PARTS_C) if c * COLS < high and (c + 1) * COLS > low]
            tile = turned[inside[0]]
            for c in inside[1:]:
                tile = jnp.where(lane >= c * COLS - low, turned[c], tile)
            if high > SIZE:
                tile = jnp.where(lane < SIZE - low, tile, jnp.zeros_like(tile))
            tiles.append(tile)
        rows.append(jnp.concatenate(tiles, axis=1))
    return jnp.concatenate(rows, axis=0)


def matrix_out(values, a, count, wide):
    lane = lax.broadcasted_iota(jnp.int32, (LANES, LANES), 1)
    stride = rows_of(count)
    height = SUBS if count == 1 else TILES
    for c in range(PARTS_C):
        low = c * COLS
        first, last = low // LANES, (low + COLS - 1) // LANES
        piece = None
        for t in range(PER):
            band = values[t * LANES : (t + 1) * LANES]
            source = band[:, first * LANES : (first + 1) * LANES]
            if last != first:
                source = jnp.where(lane >= low % LANES, source, band[:, last * LANES : (last + 1) * LANES])
            shift = ((t - c) * COLS) % LANES
            if shift:
                source = pltpu.roll(source, shift, 1)
            piece = source if piece is None else jnp.where(lane >= t * COLS, source, piece)
        piece = jnp.where(lane < PER * COLS, piece, 0.0)
        for r in range(PARTS_R):
            start = (r * PARTS_C + c) * stride + a * TILES
            wide[start : start + height, :] = piece[r * SUBS : r * SUBS + height]


def residue_of(index):
    part, s, t = (index % LANES) // SUBS, index % SUBS, index // LANES
    inner = PER * s + t
    return jnp.where((s < TILES) & (inner < ROWS), part * ROWS + inner, -1)


def first_to_second():
    first = lax.broadcasted_iota(jnp.int32, (WIDE, WIDE), 1)
    second = lax.broadcasted_iota(jnp.int32, (WIDE, WIDE), 0)
    return jnp.where(residue_of(first) == second, 1.0, 0.0).astype(BF16)


def second_to_first():
    first = lax.broadcasted_iota(jnp.int32, (WIDE, WIDE), 0)
    second = lax.broadcasted_iota(jnp.int32, (WIDE, WIDE), 1)
    return jnp.where(residue_of(first) == second, 1.0, 0.0).astype(BF16)


def edges(normed, proj_mat, kept_ref):
    projected = dot(proj_mat, normed, 0, 0)
    p1, p2, p3, p4 = [projected[q * CHANNELS : (q + 1) * CHANNELS] for q in range(4)]
    s1, s3 = sigmoid(p1), sigmoid(p3)
    left, right = s1 * p2, s3 * p4
    for q, value in enumerate((s1, left, s3, right)):
        kept_ref[q] = value
    return left, right


def back_head(upstream, gating, product, normed_mix, mix_normed, mix_inverse, out_mat):
    through = (upstream * gating).astype(BF16)
    gate_up = (upstream * product * gating * (1.0 - gating)).astype(BF16)
    mix_up = dot(out_mat, through, 1, 0)
    out_part = dot(normed_mix, through, 1, 1)
    return norm_back(mix_normed, mix_inverse, mix_up), out_part, gate_up


def back_tail(upstream, pair_normed, pair_inverse, kept_ref, left_grad, right_grad, gate_up, proj_mat, gate_mat):
    s1, left, s3, right = [kept_ref[q] for q in range(4)]
    proj_up = jnp.concatenate(
        [left_grad * left * (1.0 - s1), left_grad * s1, right_grad * right * (1.0 - s3), right_grad * s3], axis=0
    ).astype(BF16)
    normed_up = dot(proj_mat, proj_up, 1, 0) + dot(gate_mat, gate_up, 1, 0)
    return upstream + norm_back(pair_normed, pair_inverse, normed_up), proj_up


def start_kernel(pair_ref, proj_ref, message_ref, flat_ref, normed_ref, inverse_ref, kept_ref, wide):
    pair = block_in(pair_ref)
    flat_ref[...] = pair.astype(BF16)
    pair_normed, inverse = norm_parts(pair)
    normed_ref[...] = pair_normed
    inverse_ref[...] = inverse
    pack(edges(pair_normed.astype(BF16), proj_ref[0], kept_ref), message_ref, wide)


def middle_kernel(
    mix_ref, pair_ref, normed0_ref, proj_ref, gate_ref, out_ref,
    message_ref, mix_normed_ref, mix_inverse_ref, product_ref, gating0_ref, after_ref, normed_ref, inverse_ref, kept_ref,
    gating_ref, narrow, wide,
):
    (mix,) = unpack(mix_ref, narrow, 1)
    mix_normed, mix_inverse = norm_parts(mix)
    mix_normed_ref[...] = mix_normed
    mix_inverse_ref[...] = mix_inverse
    product = dot(out_ref[0], mix_normed.astype(BF16), 0, 0)
    product_ref[...] = product
    gating0 = sigmoid(dot(gate_ref[0], normed0_ref[...].astype(BF16), 0, 0))
    gating0_ref[...] = gating0
    after = (pair_ref[...].astype(F32) + gating0 * product).astype(BF16)
    after_ref[...] = after
    pair_normed, inverse = norm_parts(after.astype(F32))
    normed_ref[...] = pair_normed
    inverse_ref[...] = inverse
    normed = pair_normed.astype(BF16)
    pack(edges(normed, proj_ref[1], kept_ref), message_ref, wide)
    gating_ref[...] = sigmoid(dot(gate_ref[1], normed, 0, 0))


def turn_kernel(
    mix_ref, after_ref, gating_ref, cot_ref, out_ref, normed_ref,
    pair_out_hbm, message_ref, cot_out_ref, gate_up_ref, gate_part_ref, out_part_ref, narrow, pair_out, sem,
):
    (mix,) = unpack(mix_ref, narrow, 1)
    mix_normed, mix_inverse = norm_parts(mix)
    normed_mix = mix_normed.astype(BF16)
    product = dot(out_ref[1], normed_mix, 0, 0)
    gating = gating_ref[...]
    pair_out[...] = block_out(after_ref[...].astype(F32) + gating * product).astype(BF16)
    copy = pltpu.make_async_copy(pair_out, pair_out_hbm, sem)
    copy.start()
    cot = block_in(cot_ref)
    cot_out_ref[...] = cot.astype(BF16)
    mix_grad, out_part, gate_up = back_head(cot, gating, product, normed_mix, mix_normed, mix_inverse, out_ref[1])
    pack([mix_grad], message_ref, narrow)
    out_part_ref[...] = out_part
    gate_up_ref[...] = gate_up
    gate_part_ref[...] = dot(normed_ref[...].astype(BF16), gate_up, 1, 1)
    copy.wait()


def back_kernel(
    grads_ref, cot_ref, normed1_ref, inverse1_ref, kept1_ref, gate_up1_ref, mix_normed_ref, mix_inverse_ref,
    product_ref, gating0_ref, proj_ref, gate_ref, out_ref,
    message_ref, upstream_ref, gate_up_ref, proj_part_ref, out_part_ref, narrow, wide,
):
    left_grad, right_grad = unpack(grads_ref, wide, 2)
    pair_normed = normed1_ref[...]
    upstream, proj_up = back_tail(
        cot_ref[...].astype(F32), pair_normed, inverse1_ref[...], kept1_ref, left_grad, right_grad, gate_up1_ref[...],
        proj_ref[1], gate_ref[1],
    )
    upstream_ref[...] = upstream
    proj_part_ref[...] = dot(pair_normed.astype(BF16), proj_up, 1, 1)
    mix_normed = mix_normed_ref[...]
    mix_grad, out_part, gate_up = back_head(
        upstream, gating0_ref[...], product_ref[...], mix_normed.astype(BF16), mix_normed, mix_inverse_ref[...],
        out_ref[0],
    )
    pack([mix_grad], message_ref, narrow)
    out_part_ref[...] = out_part
    gate_up_ref[...] = gate_up


def last_kernel(
    grads_ref, upstream_ref, normed_ref, inverse_ref, kept_ref, gate_up_ref, proj_ref, gate_ref,
    proj1_ref, gate1_ref, out1_ref, out0_ref,
    pair_grad_hbm, message_ref, wide, weights, pair_grad, sem,
):
    left_grad, right_grad = unpack(grads_ref, wide, 2)
    pair_normed = normed_ref[...]
    gate_up = gate_up_ref[...]
    total, proj_up = back_tail(
        upstream_ref[...], pair_normed, inverse_ref[...], kept_ref, left_grad, right_grad, gate_up,
        proj_ref[0], gate_ref[0],
    )
    pair_grad[...] = block_out(total)
    copy = pltpu.make_async_copy(pair_grad, pair_grad_hbm, sem)
    copy.start()
    normed = pair_normed.astype(BF16)
    proj_part = dot(normed, proj_up, 1, 1)
    parts = [proj_part[:, q * LANES : (q + 1) * LANES] for q in range(4)]
    parts += [proj1_ref[:, q * LANES : (q + 1) * LANES] for q in range(4)]
    parts += [dot(normed, gate_up, 1, 1), gate1_ref[...], out0_ref[...], out1_ref[...]]
    for q, part in enumerate(parts):
        weights[pl.ds(q, CHANNELS, stride=WEIGHTS), :] = part
    message_ref[...] = weights[...].astype(BF16)
    copy.wait()


def sum_kernel(parts_ref, total_ref):
    pairs = parts_ref[...].astype(F32).reshape(DEVICES // 2, 2 * WEIGHTS, LANES)
    total = jnp.sum(pairs, axis=0)
    total = (total[:WEIGHTS] + total[WEIGHTS:]) * (1.0 / SIZE)
    total = jnp.concatenate([total, total], axis=0)[None]
    total_ref[...] = jnp.broadcast_to(total, pairs.shape).reshape(DEVICES * WEIGHTS, LANES).astype(BF16)


def spread_kernel(sums_ref, proj_hbm, gate_hbm, out_hbm, weights, proj, gate, out, sems):
    weights[...] = sums_ref[...].astype(F32)
    copies = []
    for l in range(2):
        proj[l] = jnp.concatenate(
            [weights[pl.ds(4 * l + q, CHANNELS, stride=WEIGHTS), :] for q in range(4)], axis=1
        )
        copies.append(pltpu.make_async_copy(proj.at[l], proj_hbm.at[l], sems.at[l]))
        copies[-1].start()
    for l in range(2):
        gate[l] = weights[pl.ds(8 + l, CHANNELS, stride=WEIGHTS), :]
        out[l] = weights[pl.ds(10 + l, CHANNELS, stride=WEIGHTS), :]
    copies.append(pltpu.make_async_copy(gate, gate_hbm, sems.at[2]))
    copies.append(pltpu.make_async_copy(out, out_hbm, sems.at[3]))
    for copy in copies[2:]:
        copy.start()
    for copy in copies:
        copy.wait()


def outgoing_kernel(edges_ref, mix_ref, left_ref, right_ref, double, single):
    double[: DEVICES * DOUBLE, :] = edges_ref[...].astype(F32)
    left, right = matrix_in(double, 0, 2), matrix_in(double, 1, 2)
    right = dot(first_to_second(), right, 1, 0).astype(BF16)
    left_ref[...], right_ref[...] = left, right
    matrix_out(dot(left, right, 1, 1), 0, 1, single)
    mix_ref[...] = single[...].astype(BF16)


def incoming_kernel(edges_ref, mix_ref, left_ref, right_ref, double, single):
    double[: DEVICES * DOUBLE, :] = edges_ref[...].astype(F32)
    left, right = matrix_in(double, 0, 2), matrix_in(double, 1, 2)
    left_ref[...], right_ref[...] = left, right
    turned = dot(second_to_first(), left, 1, 1).astype(BF16)
    matrix_out(dot(turned, right, 1, 0), 0, 1, single)
    mix_ref[...] = single[...].astype(BF16)


def incoming_back_kernel(grad_ref, left_ref, right_ref, grads_ref, double, single):
    single[...] = grad_ref[...].astype(F32)
    grad = dot(first_to_second(), matrix_in(single, 0, 1), 1, 0).astype(BF16)
    matrix_out(dot(right_ref[...], grad, 1, 1), 0, 2, double)
    matrix_out(dot(left_ref[...], grad, 1, 0), 1, 2, double)
    grads_ref[...] = double[: DEVICES * DOUBLE, :].astype(BF16)


def outgoing_back_kernel(grad_ref, left_ref, right_ref, grads_ref, double, single):
    single[...] = grad_ref[...].astype(F32)
    grad = matrix_in(single, 0, 1)
    matrix_out(dot(grad, right_ref[...], 1, 0), 0, 2, double)
    turned = dot(second_to_first(), grad, 1, 1).astype(BF16)
    matrix_out(dot(turned, left_ref[...], 1, 0), 1, 2, double)
    grads_ref[...] = double[: DEVICES * DOUBLE, :].astype(BF16)


SINGLE_SHAPE = (DEVICES * SINGLE, LANES)
DOUBLE_SHAPE = (DEVICES * DOUBLE, LANES)
WEIGHTS_SHAPE = (DEVICES * WEIGHTS, LANES)
BLOCK = (ROWS * COLS, CHANNELS)
FLAT = (CHANNELS, TILES * LANES)
KEPT = (4, CHANNELS, TILES * LANES)
LINE = (1, TILES * LANES)
SQUARE = (WIDE, WIDE)
WEIGHT = (CHANNELS, CHANNELS)
PROJ = (CHANNELS, 4 * CHANNELS)
DMA = pltpu.SemaphoreType.DMA


def call(kernel, name, outs, scratch, *operands, far_out=()):
    def spec(far):
        return pl.BlockSpec(memory_space=pl.ANY if far else pltpu.VMEM)

    return pl.pallas_call(
        kernel,
        out_shape=[jax.ShapeDtypeStruct(shape, kind) for shape, kind in outs],
        in_specs=[spec(False) for _ in operands],
        out_specs=[spec(position in far_out) for position in range(len(outs))],
        scratch_shapes=scratch,
        compiler_params=pltpu.CompilerParams(vmem_limit_bytes=24 * 1024 * 1024),
        name=name,
    )(*operands)


def exchange(message):
    rows = message.shape[0] // DEVICES
    shape = (DEVICES, rows, LANES)
    for low in (4, 2):
        if rows % 8 and rows % low == 0:
            shape = (DEVICES, rows // low, low, LANES)
            break
    return lax.all_to_all(message.reshape(shape), AXES, 0, 0, tiled=True).reshape(message.shape)


def local(pair_rep, proj_weight, gate_weight, out_weight, pair_cot):
    pair = pair_rep.reshape(BLOCK)
    cot = pair_cot.reshape(BLOCK)
    single, double, weights = [pltpu.VMEM(shape, F32) for shape in (SINGLE_SHAPE, DOUBLE_SHAPE, WEIGHTS_SHAPE)]
    spaced = pltpu.VMEM((DEVICES * (SINGLE + 1), LANES), F32)
    longer = pltpu.VMEM((DEVICES * DOUBLE + SUBS, LANES), F32)
    edges0, pair0, normed0, inverse0, kept0 = call(
        start_kernel, "start", [(DOUBLE_SHAPE, BF16), (FLAT, BF16), (FLAT, F32), (LINE, F32), (KEPT, F32)], [double],
        pair, proj_weight,
    )
    mix0, left0, right0 = call(
        outgoing_kernel, "outgoing", [(SINGLE_SHAPE, BF16), (SQUARE, BF16), (SQUARE, BF16)], [longer, single],
        exchange(edges0),
    )
    edges1, mix_normed0, mix_inverse0, product0, gating0, after, normed1, inverse1, kept1, gating1 = call(
        middle_kernel, "middle",
        [
            (DOUBLE_SHAPE, BF16), (FLAT, F32), (LINE, F32), (FLAT, F32), (FLAT, F32), (FLAT, BF16), (FLAT, F32),
            (LINE, F32), (KEPT, F32), (FLAT, F32),
        ],
        [spaced, double], exchange(mix0), pair0, normed0, proj_weight, gate_weight, out_weight,
    )
    mix1, left1, right1 = call(
        incoming_kernel, "incoming", [(SINGLE_SHAPE, BF16), (SQUARE, BF16), (SQUARE, BF16)], [longer, single],
        exchange(edges1),
    )
    pair_out, grad1, cot1, gate_up1, gate_part1, out_part1 = call(
        turn_kernel, "turn",
        [(BLOCK, BF16), (SINGLE_SHAPE, BF16), (FLAT, BF16), (FLAT, BF16), (WEIGHT, F32), (WEIGHT, F32)],
        [spaced, pltpu.VMEM(BLOCK, BF16), DMA],
        exchange(mix1), after, gating1, cot, out_weight, normed1, far_out=(0,),
    )
    (grads1,) = call(
        incoming_back_kernel, "incoming_back", [(DOUBLE_SHAPE, BF16)], [longer, single], exchange(grad1), left1, right1
    )
    grad0, upstream, gate_up0, proj_part1, out_part0 = call(
        back_kernel, "back",
        [(SINGLE_SHAPE, BF16), (FLAT, F32), (FLAT, BF16), (PROJ, F32), (WEIGHT, F32)],
        [spaced, double], exchange(grads1), cot1, normed1, inverse1, kept1, gate_up1, mix_normed0, mix_inverse0,
        product0, gating0, proj_weight, gate_weight, out_weight,
    )
    (grads0,) = call(
        outgoing_back_kernel, "outgoing_back", [(DOUBLE_SHAPE, BF16)], [longer, single], exchange(grad0), left0, right0
    )
    pair_grad, parts = call(
        last_kernel, "last", [(BLOCK, F32), (WEIGHTS_SHAPE, BF16)],
        [double, weights, pltpu.VMEM(BLOCK, F32), DMA],
        exchange(grads0), upstream, normed0, inverse0, kept0, gate_up0, proj_weight, gate_weight,
        proj_part1, gate_part1, out_part1, out_part0, far_out=(0,),
    )
    (sums,) = call(sum_kernel, "sum", [(WEIGHTS_SHAPE, BF16)], [], exchange(parts))
    proj_grad, gate_grad, out_grad = call(
        spread_kernel, "spread", [((2,) + PROJ, F32), ((2,) + WEIGHT, F32), ((2,) + WEIGHT, F32)],
        [weights, pltpu.VMEM((2,) + PROJ, F32), pltpu.VMEM((2,) + WEIGHT, F32), pltpu.VMEM((2,) + WEIGHT, F32), DMA((4,))],
        exchange(sums), far_out=(0, 1, 2),
    )
    return (
        pair_out.reshape(ROWS, COLS, CHANNELS),
        pair_grad.reshape(ROWS, COLS, CHANNELS),
        proj_grad,
        gate_grad,
        out_grad,
    )


def solution(mesh):
    in_specs = (P("row", "col", None), P(), P(), P(), P("row", "col", None))
    out_specs = (P("row", "col", None), P("row", "col", None), P(), P(), P())
    return jax.shard_map(local, mesh=mesh, in_specs=in_specs, out_specs=out_specs, check_vma=False)
```

time: 190 us -> 183 us (0.963)
  blocking collectives: 173 us -> 168 us
  Pallas kernels: 13.6 us -> 11.7 us
    all_to_all x10, blocking collectives: 173 us -> 168 us  [exchange(): lax.all_to_all(message.reshape(shape), AXES, 0, 0, tiled=True)]
    pallas_call x11, Pallas kernels: 13.6 us -> 11.7 us  [call(): pl.pallas_call(kernel, out_shape=[jax.ShapeDtypeStruct(shape, kind) for s...]
where the time goes in v2:
time: 183 us; the launch traced here: 182 us
  blocking collectives  168 us (92%)
  Pallas kernels  11.7 us (6%)
  local copies, waits for them, and re-layouts  1.89 us (1%)
    all_to_all x10, blocking collectives, exchange(): lax.all_to_all(message.reshape(shape), AXES, 0, 0, tiled=True)  168 us
    pallas_call x11, Pallas kernels, call(): pl.pallas_call(kernel, out_shape=[jax.ShapeDtypeStruct(shape, kind) for s...  11.7 us

profile of v2, /device:TPU:1, one launch (start us, length us, event | category | flops | bytes accessed | tf_op | source)
XLA Modules:
  0.0 182.3 jit_solution(1761378497226795312)
XLA Ops:
  0.6 0.9 copy-done
  1.6 0.9 copy-done.5
  2.5 0.6 start.1
  3.1 23.7 %all_to_all.50 = bf16[128,7,2,128]{3,2,1,0:T(2,128)(2,1)S(1)} all-to-all(bf16[128,7,2,128]{3,2,1,0:T(2,128)(2,1)S(1)} %bitcast.38), channel_id=1, replica_groups=mesh['row'=16,'col'=8] {'row','col'}, dimensions={0} | all-to-all | bytes 917504 | tf_op jit(solution)/shard_map/all_to_all | solution.py:407
  26.8 1.0 outgoing.1
  27.9 0.0 copy-start.4
  27.9 15.5 %all_to_all.51 = bf16[128,8,128]{2,1,0:T(8,128)(2,1)S(1)} all-to-all(bf16[128,8,128]{2,1,0:T(8,128)(2,1)S(1)} %bitcast.42), channel_id=1, replica_groups=mesh['row'=16,'col'=8] {'row','col'}, dimensions={0} | all-to-all | bytes 524288 | tf_op jit(solution)/shard_map/all_to_all | solution.py:407
  43.4 1.1 middle.1
  44.5 16.5 %all_to_all.52 = bf16[128,7,2,128]{3,2,1,0:T(2,128)(2,1)S(1)} all-to-all(bf16[128,7,2,128]{3,2,1,0:T(2,128)(2,1)S(1)} %bitcast.37), channel_id=1, replica_groups=mesh['row'=16,'col'=8] {'row','col'}, dimensions={0} | all-to-all | bytes 917504 | tf_op jit(solution)/shard_map/all_to_all | solution.py:407
  61.0 1.0 incoming.1
  62.0 15.5 %all_to_all.53 = bf16[128,8,128]{2,1,0:T(8,128)(2,1)S(1)} all-to-all(bf16[128,8,128]{2,1,0:T(8,128)(2,1)S(1)} %bitcast.43), channel_id=1, replica_groups=mesh['row'=16,'col'=8] {'row','col'}, dimensions={0} | all-to-all | bytes 524288 | tf_op jit(solution)/shard_map/all_to_all | solution.py:407
  77.5 1.4 turn.1
  78.9 15.1 %all_to_all.54 = bf16[128,8,128]{2,1,0:T(8,128)(2,1)S(1)} all-to-all(bf16[128,8,128]{2,1,0:T(8,128)(2,1)S(1)} %bitcast.41), channel_id=1, replica_groups=mesh['row'=16,'col'=8] {'row','col'}, dimensions={0} | all-to-all | bytes 524288 | tf_op jit(solution)/shard_map/all_to_all | solution.py:407
  94.0 1.5 incoming_back.1
  95.5 16.5 %all_to_all.55 = bf16[128,7,2,128]{3,2,1,0:T(2,128)(2,1)S(1)} all-to-all(bf16[128,7,2,128]{3,2,1,0:T(2,128)(2,1)S(1)} %bitcast.26), channel_id=1, replica_groups=mesh['row'=16,'col'=8] {'row','col'}, dimensions={0} | all-to-all | bytes 917504 | tf_op jit(solution)/shard_map/all_to_all | solution.py:407
  112.1 1.0 back.1
  113.1 15.5 %all_to_all.56 = bf16[128,8,128]{2,1,0:T(8,128)(2,1)S(1)} all-to-all(bf16[128,8,128]{2,1,0:T(8,128)(2,1)S(1)} %bitcast.40), channel_id=1, replica_groups=mesh['row'=16,'col'=8] {'row','col'}, dimensions={0} | all-to-all | bytes 524288 | tf_op jit(solution)/shard_map/all_to_all | solution.py:407
  128.6 1.4 outgoing_back.1
  130.1 16.5 %all_to_all.57 = bf16[128,7,2,128]{3,2,1,0:T(2,128)(2,1)S(1)} all-to-all(bf16[128,7,2,128]{3,2,1,0:T(2,128)(2,1)S(1)} %bitcast.27), channel_id=1, replica_groups=mesh['row'=16,'col'=8] {'row','col'}, dimensions={0} | all-to-all | bytes 917504 | tf_op jit(solution)/shard_map/all_to_all | solution.py:407
  146.6 1.6 last.1
  148.2 16.5 %all_to_all.58 = bf16[128,3,4,128]{3,2,1,0:T(4,128)(2,1)S(1)} all-to-all(bf16[128,3,4,128]{3,2,1,0:T(4,128)(2,1)S(1)} %bitcast.39), channel_id=1, replica_groups=mesh['row'=16,'col'=8] {'row','col'}, dimensions={0} | all-to-all | bytes 786432 | tf_op jit(solution)/shard_map/all_to_all | solution.py:407
  164.7 0.1 sum.1
  164.8 16.4 %all_to_all.59 = bf16[128,3,4,128]{3,2,1,0:T(4,128)(2,1)S(1)} all-to-all(bf16[128,3,4,128]{3,2,1,0:T(4,128)(2,1)S(1)} %bitcast.32), channel_id=1, replica_groups=mesh['row'=16,'col'=8] {'row','col'}, dimensions={0} | all-to-all | bytes 786432 | tf_op jit(solution)/shard_map/all_to_all | solution.py:407
  181.1 1.0 spread.1
  (9 shorter events, 0.0 us)
Async XLA Ops:
  0.6 1.0 copy-start
  1.6 0.9 copy-start.5
  2.5 40.9 %copy-start.1 = (bf16[2,128,512]{2,1,0:T(8,128)(2,1)S(1)}, bf16[2,128,512]{2,1,0:T(8,128)(2,1)}, u32[]{:S(2)}) copy-start(bf16[2,128,512]{2,1,0:T(8,128)(2,1)} %proj_ref.7) | copy-start | bytes 786436
  2.5 40.9 %copy-start.2 = (bf16[2,128,128]{2,1,0:T(8,128)(2,1)S(1)}, bf16[2,128,128]{2,1,0:T(8,128)(2,1)}, u32[]{:S(2)}) copy-start(bf16[2,128,128]{2,1,0:T(8,128)(2,1)} %gate_ref.5) | copy-start | bytes 196612
  2.5 40.9 %copy-start.3 = (bf16[2,128,128]{2,1,0:T(8,128)(2,1)S(1)}, bf16[2,128,128]{2,1,0:T(8,128)(2,1)}, u32[]{:S(2)}) copy-start(bf16[2,128,128]{2,1,0:T(8,128)(2,1)} %out_ref.5) | copy-start | bytes 196612
  27.9 49.7 %copy-start.4 = (bf16[20,40,128]{2,1,0:T(8,128)(2,1)S(1)}, bf16[20,40,128]{2,1,0:T(8,128)(2,1)}, u32[]{:S(2)}) copy-start(bf16[20,40,128]{2,1,0:T(8,128)(2,1)} %param.9) | copy-start | bytes 614404

commit v3 on v2

--- a/solution.py
+++ b/solution.py
@@ -49,16 +49,20 @@
     return 0.5 * jnp.tanh(0.5 * values) + 0.5
 
 
+def identity():
+    shape = (CHANNELS, CHANNELS)
+    same = lax.broadcasted_iota(jnp.int32, shape, 0) == lax.broadcasted_iota(jnp.int32, shape, 1)
+    return jnp.where(same, 1.0, 0.0).astype(BF16)
+
+
 def block_in(ref):
     values = ref[...].astype(F32)
-    tiles = []
+    pieces = []
     for s in range(TILES):
         low = s * PER * COLS
         high = min(low + PER * COLS, ROWS * COLS)
-        piece = values[low:high]
-        piece = jnp.concatenate([piece, jnp.zeros((LANES - (high - low), CHANNELS), F32)], axis=0)
-        tiles.append(piece.T)
-    return jnp.concatenate(tiles, axis=1)
+        pieces += [values[low:high], jnp.zeros((LANES - (high - low), CHANNELS), F32)]
+    return dot(identity(), jnp.concatenate(pieces, axis=0).astype(BF16), 1, 1)
 
 
 def block_out(values):
@@ -67,6 +71,14 @@
         count = min(PER * COLS, ROWS * COLS - s * PER * COLS)
         pieces.append(values[:, s * LANES : (s + 1) * LANES].T[:count])
     return jnp.concatenate(pieces, axis=0)
+
+
+def block_out_exact(values):
+    pieces = []
+    for s in range(TILES):
+        count = min(PER * COLS, ROWS * COLS - s * PER * COLS)
+        pieces.append(dot(identity(), values[:, s * LANES : (s + 1) * LANES], 1, 1)[:count])
+    return jnp.concatenate(pieces, axis=0).astype(BF16)
 
 
 def rows_of(parts):
@@ -106,15 +118,28 @@
     ]
 
 
-def matrix_in(wide, a, count):
+def pieces_in(ref, count):
+    values = ref[...].astype(F32).reshape(PARTS_R, -1, SUBS, LANES)
+    if count == 1:
+        return [[values[:, c].reshape(LANES, LANES) for c in range(PARTS_C)]]
+    sub = lax.broadcasted_iota(jnp.int32, (PARTS_R, SUBS, LANES), 1)
+    parts = []
+    for a in range(count):
+        parts.append([])
+        for c in range(PARTS_C):
+            tile, shift = divmod(c * DOUBLE + a * TILES, SUBS)
+            piece = values[:, tile]
+            if shift + TILES > SUBS:
+                piece = jnp.where(sub >= shift, piece, values[:, tile + 1])
+            if shift:
+                piece = pltpu.roll(piece, SUBS - shift, 1)
+            parts[a].append(jnp.where(sub < TILES, piece, 0.0).reshape(LANES, LANES))
+    return parts
+
+
+def matrix_of(pieces):
     lane = lax.broadcasted_iota(jnp.int32, (LANES, LANES), 1)
-    real = lax.broadcasted_iota(jnp.int32, (LANES, LANES), 0) % SUBS < TILES
-    stride = rows_of(count)
-    pieces = []
-    for c in range(PARTS_C):
-        starts = [(r * PARTS_C + c) * stride + a * TILES for r in range(PARTS_R)]
-        piece = jnp.concatenate([wide[start : start + SUBS, :] for start in starts], axis=0)
-        pieces.append((piece if count == 1 else jnp.where(real, piece, 0.0)).astype(BF16))
+    pieces = [piece.astype(BF16) for piece in pieces]
     rows = []
     for t in range(PER):
         turned = [
@@ -135,10 +160,9 @@
     return jnp.concatenate(rows, axis=0)
 
 
-def matrix_out(values, a, count, wide):
+def pieces_of(values):
     lane = lax.broadcasted_iota(jnp.int32, (LANES, LANES), 1)
-    stride = rows_of(count)
-    height = SUBS if count == 1 else TILES
+    pieces = []
     for c in range(PARTS_C):
         low = c * COLS
         first, last = low // LANES, (low + COLS - 1) // LANES
@@ -152,28 +176,45 @@
             if shift:
                 source = pltpu.roll(source, shift, 1)
             piece = source if piece is None else jnp.where(lane >= t * COLS, source, piece)
-        piece = jnp.where(lane < PER * COLS, piece, 0.0)
-        for r in range(PARTS_R):
-            start = (r * PARTS_C + c) * stride + a * TILES
-            wide[start : start + height, :] = piece[r * SUBS : r * SUBS + height]
-
-
-def residue_of(index):
+        pieces.append(jnp.where(lane < PER * COLS, piece, 0.0))
+    return pieces
+
+
+def pieces_out(parts, ref):
+    if len(parts) == 1:
+        tiles = [piece.reshape(PARTS_R, SUBS, LANES) for piece in parts[0]]
+    else:
+        sub = lax.broadcasted_iota(jnp.int32, (PARTS_R, SUBS, LANES), 1)
+        tiles = [None] * (PARTS_C * DOUBLE // SUBS)
+        for c in range(PARTS_C):
+            for a, pieces in enumerate(parts):
+                tile, shift = divmod(c * DOUBLE + a * TILES, SUBS)
+                piece = pieces[c].reshape(PARTS_R, SUBS, LANES)
+                if shift:
+                    piece = pltpu.roll(piece, shift, 1)
+                tiles[tile] = piece if tiles[tile] is None else jnp.where(sub >= shift, piece, tiles[tile])
+                if shift + TILES > SUBS:
+                    tiles[tile + 1] = piece
+    values = jnp.concatenate([tile[:, None] for tile in tiles], axis=1)
+    ref[...] = values.reshape(-1, LANES).astype(BF16)
+
+
+def first_to_second():
+    index = lax.broadcasted_iota(jnp.int32, (1, WIDE), 1)
     part, s, t = (index % LANES) // SUBS, index % SUBS, index // LANES
     inner = PER * s + t
-    return jnp.where((s < TILES) & (inner < ROWS), part * ROWS + inner, -1)
-
-
-def first_to_second():
-    first = lax.broadcasted_iota(jnp.int32, (WIDE, WIDE), 1)
+    residue = jnp.where((s < TILES) & (inner < ROWS), part * ROWS + inner, -1)
     second = lax.broadcasted_iota(jnp.int32, (WIDE, WIDE), 0)
-    return jnp.where(residue_of(first) == second, 1.0, 0.0).astype(BF16)
+    return jnp.where(second == residue, 1.0, 0.0).astype(BF16)
 
 
 def second_to_first():
-    first = lax.broadcasted_iota(jnp.int32, (WIDE, WIDE), 0)
+    index = lax.broadcasted_iota(jnp.int32, (WIDE, 1), 0)
+    part, s, t = (index % LANES) // SUBS, index % SUBS, index // LANES
+    inner = PER * s + t
+    residue = jnp.where((s < TILES) & (inner < ROWS), part * ROWS + inner, -1)
     second = lax.broadcasted_iota(jnp.int32, (WIDE, WIDE), 1)
-    return jnp.where(residue_of(first) == second, 1.0, 0.0).astype(BF16)
+    return jnp.where(second == residue, 1.0, 0.0).astype(BF16)
 
 
 def edges(normed, proj_mat, kept_ref):
@@ -244,7 +285,7 @@
     normed_mix = mix_normed.astype(BF16)
     product = dot(out_ref[1], normed_mix, 0, 0)
     gating = gating_ref[...]
-    pair_out[...] = block_out(after_ref[...].astype(F32) + gating * product).astype(BF16)
+    pair_out[...] = block_out_exact((after_ref[...].astype(F32) + gating * product).astype(BF16))
     copy = pltpu.make_async_copy(pair_out, pair_out_hbm, sem)
     copy.start()
     cot = block_in(cot_ref)
@@ -283,7 +324,7 @@
 def last_kernel(
     grads_ref, upstream_ref, normed_ref, inverse_ref, kept_ref, gate_up_ref, proj_ref, gate_ref,
     proj1_ref, gate1_ref, out1_ref, out0_ref,
-    pair_grad_hbm, message_ref, wide, weights, pair_grad, sem,
+    pair_grad_hbm, message_ref, wide, pair_grad, sem,
 ):
     left_grad, right_grad = unpack(grads_ref, wide, 2)
     pair_normed = normed_ref[...]
@@ -301,8 +342,7 @@
     parts += [proj1_ref[:, q * LANES : (q + 1) * LANES] for q in range(4)]
     parts += [dot(normed, gate_up, 1, 1), gate1_ref[...], out0_ref[...], out1_ref[...]]
     for q, part in enumerate(parts):
-        weights[pl.ds(q, CHANNELS, stride=WEIGHTS), :] = part
-    message_ref[...] = weights[...].astype(BF16)
+        message_ref[q * CHANNELS : (q + 1) * CHANNELS, :] = part.astype(BF16)
     copy.wait()
 
 
@@ -314,18 +354,15 @@
     total_ref[...] = jnp.broadcast_to(total, pairs.shape).reshape(DEVICES * WEIGHTS, LANES).astype(BF16)
 
 
-def spread_kernel(sums_ref, proj_hbm, gate_hbm, out_hbm, weights, proj, gate, out, sems):
-    weights[...] = sums_ref[...].astype(F32)
+def spread_kernel(sums_ref, proj_hbm, gate_hbm, out_hbm, proj, gate, out, sems):
+    parts = [sums_ref[q * CHANNELS : (q + 1) * CHANNELS, :].astype(F32) for q in range(WEIGHTS)]
     copies = []
     for l in range(2):
-        proj[l] = jnp.concatenate(
-            [weights[pl.ds(4 * l + q, CHANNELS, stride=WEIGHTS), :] for q in range(4)], axis=1
-        )
+        proj[l] = jnp.concatenate(parts[4 * l : 4 * l + 4], axis=1)
         copies.append(pltpu.make_async_copy(proj.at[l], proj_hbm.at[l], sems.at[l]))
         copies[-1].start()
     for l in range(2):
-        gate[l] = weights[pl.ds(8 + l, CHANNELS, stride=WEIGHTS), :]
-        out[l] = weights[pl.ds(10 + l, CHANNELS, stride=WEIGHTS), :]
+        gate[l], out[l] = parts[8 + l], parts[10 + l]
     copies.append(pltpu.make_async_copy(gate, gate_hbm, sems.at[2]))
     copies.append(pltpu.make_async_copy(out, out_hbm, sems.at[3]))
     for copy in copies[2:]:
@@ -334,39 +371,33 @@
         copy.wait()
 
 
-def outgoing_kernel(edges_ref, mix_ref, left_ref, right_ref, double, single):
-    double[: DEVICES * DOUBLE, :] = edges_ref[...].astype(F32)
-    left, right = matrix_in(double, 0, 2), matrix_in(double, 1, 2)
-    right = dot(first_to_second(), right, 1, 0).astype(BF16)
+def outgoing_kernel(edges_ref, mix_ref, left_ref, right_ref, forth_ref):
+    forth = first_to_second()
+    forth_ref[...] = forth
+    left, right = [matrix_of(pieces) for pieces in pieces_in(edges_ref, 2)]
+    right = dot(forth, right, 1, 0).astype(BF16)
     left_ref[...], right_ref[...] = left, right
-    matrix_out(dot(left, right, 1, 1), 0, 1, single)
-    mix_ref[...] = single[...].astype(BF16)
-
-
-def incoming_kernel(edges_ref, mix_ref, left_ref, right_ref, double, single):
-    double[: DEVICES * DOUBLE, :] = edges_ref[...].astype(F32)
-    left, right = matrix_in(double, 0, 2), matrix_in(double, 1, 2)
+    pieces_out([pieces_of(dot(left, right, 1, 1))], mix_ref)
+
+
+def incoming_kernel(edges_ref, mix_ref, left_ref, right_ref, back_ref):
+    back = second_to_first()
+    back_ref[...] = back
+    left, right = [matrix_of(pieces) for pieces in pieces_in(edges_ref, 2)]
     left_ref[...], right_ref[...] = left, right
-    turned = dot(second_to_first(), left, 1, 1).astype(BF16)
-    matrix_out(dot(turned, right, 1, 0), 0, 1, single)
-    mix_ref[...] = single[...].astype(BF16)
-
-
-def incoming_back_kernel(grad_ref, left_ref, right_ref, grads_ref, double, single):
-    single[...] = grad_ref[...].astype(F32)
-    grad = dot(first_to_second(), matrix_in(single, 0, 1), 1, 0).astype(BF16)
-    matrix_out(dot(right_ref[...], grad, 1, 1), 0, 2, double)
-    matrix_out(dot(left_ref[...], grad, 1, 0), 1, 2, double)
-    grads_ref[...] = double[: DEVICES * DOUBLE, :].astype(BF16)
-
-
-def outgoing_back_kernel(grad_ref, left_ref, right_ref, grads_ref, double, single):
-    single[...] = grad_ref[...].astype(F32)
-    grad = matrix_in(single, 0, 1)
-    matrix_out(dot(grad, right_ref[...], 1, 0), 0, 2, double)
-    turned = dot(second_to_first(), grad, 1, 1).astype(BF16)
-    matrix_out(dot(turned, left_ref[...], 1, 0), 1, 2, double)
-    grads_ref[...] = double[: DEVICES * DOUBLE, :].astype(BF16)
+    turned = dot(back, left, 1, 1).astype(BF16)
+    pieces_out([pieces_of(dot(turned, right, 1, 0))], mix_ref)
+
+
+def incoming_back_kernel(grad_ref, forth_ref, left_ref, right_ref, grads_ref):
+    grad = dot(forth_ref[...], matrix_of(pieces_in(grad_ref, 1)[0]), 1, 0).astype(BF16)
+    pieces_out([pieces_of(dot(right_ref[...], grad, 1, 1)), pieces_of(dot(left_ref[...], grad, 1, 0))], grads_ref)
+
+
+def outgoing_back_kernel(grad_ref, back_ref, left_ref, right_ref, grads_ref):
+    grad = matrix_of(pieces_in(grad_ref, 1)[0])
+    turned = dot(back_ref[...], grad, 1, 1).astype(BF16)
+    pieces_out([pieces_of(dot(grad, right_ref[...], 1, 0)), pieces_of(dot(turned, left_ref[...], 1, 0))], grads_ref)
 
 
 SINGLE_SHAPE = (DEVICES * SINGLE, LANES)
@@ -410,15 +441,14 @@
 def local(pair_rep, proj_weight, gate_weight, out_weight, pair_cot):
     pair = pair_rep.reshape(BLOCK)
     cot = pair_cot.reshape(BLOCK)
-    single, double, weights = [pltpu.VMEM(shape, F32) for shape in (SINGLE_SHAPE, DOUBLE_SHAPE, WEIGHTS_SHAPE)]
+    double = pltpu.VMEM(DOUBLE_SHAPE, F32)
     spaced = pltpu.VMEM((DEVICES * (SINGLE + 1), LANES), F32)
-    longer = pltpu.VMEM((DEVICES * DOUBLE + SUBS, LANES), F32)
     edges0, pair0, normed0, inverse0, kept0 = call(
         start_kernel, "start", [(DOUBLE_SHAPE, BF16), (FLAT, BF16), (FLAT, F32), (LINE, F32), (KEPT, F32)], [double],
         pair, proj_weight,
     )
-    mix0, left0, right0 = call(
-        outgoing_kernel, "outgoing", [(SINGLE_SHAPE, BF16), (SQUARE, BF16), (SQUARE, BF16)], [longer, single],
+    mix0, left0, right0, forth = call(
+        outgoing_kernel, "outgoing", [(SINGLE_SHAPE, BF16), (SQUARE, BF16), (SQUARE, BF16), (SQUARE, BF16)], [],
         exchange(edges0),
     )
     edges1, mix_normed0, mix_inverse0, product0, gating0, after, normed1, inverse1, kept1, gating1 = call(
@@ -429,8 +459,8 @@
         ],
         [spaced, double], exchange(mix0), pair0, normed0, proj_weight, gate_weight, out_weight,
     )
-    mix1, left1, right1 = call(
-        incoming_kernel, "incoming", [(SINGLE_SHAPE, BF16), (SQUARE, BF16), (SQUARE, BF16)], [longer, single],
+    mix1, left1, right1, back = call(
+        incoming_kernel, "incoming", [(SINGLE_SHAPE, BF16), (SQUARE, BF16), (SQUARE, BF16), (SQUARE, BF16)], [],
         exchange(edges1),
     )
     pair_out, grad1, cot1, gate_up1, gate_part1, out_part1 = call(
@@ -440,7 +470,7 @@
         exchange(mix1), after, gating1, cot, out_weight, normed1, far_out=(0,),
     )
     (grads1,) = call(
-        incoming_back_kernel, "incoming_back", [(DOUBLE_SHAPE, BF16)], [longer, single], exchange(grad1), left1, right1
+        incoming_back_kernel, "incoming_back", [(DOUBLE_SHAPE, BF16)], [], exchange(grad1), forth, left1, right1
     )
     grad0, upstream, gate_up0, proj_part1, out_part0 = call(
         back_kernel, "back",
@@ -449,18 +479,18 @@
         product0, gating0, proj_weight, gate_weight, out_weight,
     )
     (grads0,) = call(
-        outgoing_back_kernel, "outgoing_back", [(DOUBLE_SHAPE, BF16)], [longer, single], exchange(grad0), left0, right0
+        outgoing_back_kernel, "outgoing_back", [(DOUBLE_SHAPE, BF16)], [], exchange(grad0), back, left0, right0
     )
     pair_grad, parts = call(
         last_kernel, "last", [(BLOCK, F32), (WEIGHTS_SHAPE, BF16)],
-        [double, weights, pltpu.VMEM(BLOCK, F32), DMA],
+        [double, pltpu.VMEM(BLOCK, F32), DMA],
         exchange(grads0), upstream, normed0, inverse0, kept0, gate_up0, proj_weight, gate_weight,
         proj_part1, gate_part1, out_part1, out_part0, far_out=(0,),
     )
     (sums,) = call(sum_kernel, "sum", [(WEIGHTS_SHAPE, BF16)], [], exchange(parts))
     proj_grad, gate_grad, out_grad = call(
         spread_kernel, "spread", [((2,) + PROJ, F32), ((2,) + WEIGHT, F32), ((2,) + WEIGHT, F32)],
-        [weights, pltpu.VMEM((2,) + PROJ, F32), pltpu.VMEM((2,) + WEIGHT, F32), pltpu.VMEM((2,) + WEIGHT, F32), DMA((4,))],
+        [pltpu.VMEM((2,) + PROJ, F32), pltpu.VMEM((2,) + WEIGHT, F32), pltpu.VMEM((2,) + WEIGHT, F32), DMA((4,))],
         exchange(sums), far_out=(0, 1, 2),
     )
     return (

time: 183 us -> 182 us (level)
  no operation moved by 1% of the time
where the time goes in v3:
time: 182 us
  blocking collectives  168 us (92%)
  Pallas kernels  11.1 us (6%)
  local copies, waits for them, and re-layouts  1.89 us (1%)
    all_to_all x10, blocking collectives, exchange(): lax.all_to_all(message.reshape(shape), AXES, 0, 0, tiled=True)  168 us
    pallas_call x11, Pallas kernels, call(): pl.pallas_call(kernel, out_shape=[jax.ShapeDtypeStruct(shape, kind) for s...  11.1 us

profile of v3, /device:TPU:1, one launch (start us, length us, event | category | flops | bytes accessed | tf_op | source)
XLA Modules:
  0.0 181.7 jit_solution(15770471655264260387)
XLA Ops:
  0.6 0.9 copy-done
  1.6 0.9 copy-done.5
  2.5 0.7 start.1
  3.2 23.7 %all_to_all.50 = bf16[128,7,2,128]{3,2,1,0:T(2,128)(2,1)S(1)} all-to-all(bf16[128,7,2,128]{3,2,1,0:T(2,128)(2,1)S(1)} %bitcast.38), channel_id=1, replica_groups=mesh['row'=16,'col'=8] {'row','col'}, dimensions={0} | all-to-all | bytes 917504 | tf_op jit(solution)/shard_map/all_to_all | solution.py:438
  26.9 1.1 outgoing.1
  28.0 0.0 copy-start.4
  28.0 15.5 %all_to_all.51 = bf16[128,8,128]{2,1,0:T(8,128)(2,1)S(1)} all-to-all(bf16[128,8,128]{2,1,0:T(8,128)(2,1)S(1)} %bitcast.42), channel_id=1, replica_groups=mesh['row'=16,'col'=8] {'row','col'}, dimensions={0} | all-to-all | bytes 524288 | tf_op jit(solution)/shard_map/all_to_all | solution.py:438
  43.6 1.1 middle.1
  44.6 16.5 %all_to_all.52 = bf16[128,7,2,128]{3,2,1,0:T(2,128)(2,1)S(1)} all-to-all(bf16[128,7,2,128]{3,2,1,0:T(2,128)(2,1)S(1)} %bitcast.37), channel_id=1, replica_groups=mesh['row'=16,'col'=8] {'row','col'}, dimensions={0} | all-to-all | bytes 917504 | tf_op jit(solution)/shard_map/all_to_all | solution.py:438
  61.2 1.0 incoming.1
  62.2 15.5 %all_to_all.53 = bf16[128,8,128]{2,1,0:T(8,128)(2,1)S(1)} all-to-all(bf16[128,8,128]{2,1,0:T(8,128)(2,1)S(1)} %bitcast.43), channel_id=1, replica_groups=mesh['row'=16,'col'=8] {'row','col'}, dimensions={0} | all-to-all | bytes 524288 | tf_op jit(solution)/shard_map/all_to_all | solution.py:438
  77.7 1.2 turn.1
  79.0 15.1 %all_to_all.54 = bf16[128,8,128]{2,1,0:T(8,128)(2,1)S(1)} all-to-all(bf16[128,8,128]{2,1,0:T(8,128)(2,1)S(1)} %bitcast.41), channel_id=1, replica_groups=mesh['row'=16,'col'=8] {'row','col'}, dimensions={0} | all-to-all | bytes 524288 | tf_op jit(solution)/shard_map/all_to_all | solution.py:438
  94.0 1.2 incoming_back.1
  95.3 16.5 %all_to_all.55 = bf16[128,7,2,128]{3,2,1,0:T(2,128)(2,1)S(1)} all-to-all(bf16[128,7,2,128]{3,2,1,0:T(2,128)(2,1)S(1)} %bitcast.28), channel_id=1, replica_groups=mesh['row'=16,'col'=8] {'row','col'}, dimensions={0} | all-to-all | bytes 917504 | tf_op jit(solution)/shard_map/all_to_all | solution.py:438
  111.8 1.0 back.1
  112.8 15.5 %all_to_all.56 = bf16[128,8,128]{2,1,0:T(8,128)(2,1)S(1)} all-to-all(bf16[128,8,128]{2,1,0:T(8,128)(2,1)S(1)} %bitcast.40), channel_id=1, replica_groups=mesh['row'=16,'col'=8] {'row','col'}, dimensions={0} | all-to-all | bytes 524288 | tf_op jit(solution)/shard_map/all_to_all | solution.py:438
  128.4 1.2 outgoing_back.1
  129.5 16.5 %all_to_all.57 = bf16[128,7,2,128]{3,2,1,0:T(2,128)(2,1)S(1)} all-to-all(bf16[128,7,2,128]{3,2,1,0:T(2,128)(2,1)S(1)} %bitcast.29), channel_id=1, replica_groups=mesh['row'=16,'col'=8] {'row','col'}, dimensions={0} | all-to-all | bytes 917504 | tf_op jit(solution)/shard_map/all_to_all | solution.py:438
  146.1 1.6 last.1
  147.6 16.5 %all_to_all.58 = bf16[128,3,4,128]{3,2,1,0:T(4,128)(2,1)S(1)} all-to-all(bf16[128,3,4,128]{3,2,1,0:T(4,128)(2,1)S(1)} %bitcast.39), channel_id=1, replica_groups=mesh['row'=16,'col'=8] {'row','col'}, dimensions={0} | all-to-all | bytes 786432 | tf_op jit(solution)/shard_map/all_to_all | solution.py:438
  164.2 0.1 sum.1
  164.3 16.4 %all_to_all.59 = bf16[128,3,4,128]{3,2,1,0:T(4,128)(2,1)S(1)} all-to-all(bf16[128,3,4,128]{3,2,1,0:T(4,128)(2,1)S(1)} %bitcast.32), channel_id=1, replica_groups=mesh['row'=16,'col'=8] {'row','col'}, dimensions={0} | all-to-all | bytes 786432 | tf_op jit(solution)/shard_map/all_to_all | solution.py:438
  180.6 0.9 spread.1
  (9 shorter events, 0.0 us)
Async XLA Ops:
  0.6 1.0 copy-start
  1.6 0.9 copy-start.5
  2.5 41.0 %copy-start.1 = (bf16[2,128,512]{2,1,0:T(8,128)(2,1)S(1)}, bf16[2,128,512]{2,1,0:T(8,128)(2,1)}, u32[]{:S(2)}) copy-start(bf16[2,128,512]{2,1,0:T(8,128)(2,1)} %proj_ref.7) | copy-start | bytes 786436
  2.5 41.0 %copy-start.2 = (bf16[2,128,128]{2,1,0:T(8,128)(2,1)S(1)}, bf16[2,128,128]{2,1,0:T(8,128)(2,1)}, u32[]{:S(2)}) copy-start(bf16[2,128,128]{2,1,0:T(8,128)(2,1)} %gate_ref.5) | copy-start | bytes 196612
  2.5 41.0 %copy-start.3 = (bf16[2,128,128]{2,1,0:T(8,128)(2,1)S(1)}, bf16[2,128,128]{2,1,0:T(8,128)(2,1)}, u32[]{:S(2)}) copy-start(bf16[2,128,128]{2,1,0:T(8,128)(2,1)} %out_ref.5) | copy-start | bytes 196612
  28.0 49.7 %copy-start.4 = (bf16[20,40,128]{2,1,0:T(8,128)(2,1)S(1)}, bf16[20,40,128]{2,1,0:T(8,128)(2,1)}, u32[]{:S(2)}) copy-start(bf16[20,40,128]{2,1,0:T(8,128)(2,1)} %param.9) | copy-start | bytes 614404

commit v4 on v3

--- a/solution.py
+++ b/solution.py
@@ -63,14 +63,6 @@
         high = min(low + PER * COLS, ROWS * COLS)
         pieces += [values[low:high], jnp.zeros((LANES - (high - low), CHANNELS), F32)]
     return dot(identity(), jnp.concatenate(pieces, axis=0).astype(BF16), 1, 1)
-
-
-def block_out(values):
-    pieces = []
-    for s in range(TILES):
-        count = min(PER * COLS, ROWS * COLS - s * PER * COLS)
-        pieces.append(values[:, s * LANES : (s + 1) * LANES].T[:count])
-    return jnp.concatenate(pieces, axis=0)
 
 
 def block_out_exact(values):
@@ -161,6 +153,7 @@
 
 
 def pieces_of(values):
+    values = values.astype(BF16)
     lane = lax.broadcasted_iota(jnp.int32, (LANES, LANES), 1)
     pieces = []
     for c in range(PARTS_C):
@@ -176,7 +169,7 @@
             if shift:
                 source = pltpu.roll(source, shift, 1)
             piece = source if piece is None else jnp.where(lane >= t * COLS, source, piece)
-        pieces.append(jnp.where(lane < PER * COLS, piece, 0.0))
+        pieces.append(jnp.where(lane < PER * COLS, piece, jnp.zeros_like(piece)).astype(F32))
     return pieces
 
 
@@ -244,7 +237,7 @@
     return upstream + norm_back(pair_normed, pair_inverse, normed_up), proj_up
 
 
-def start_kernel(pair_ref, proj_ref, message_ref, flat_ref, normed_ref, inverse_ref, kept_ref, wide):
+def start_kernel(pair_ref, proj_ref, _, message_ref, flat_ref, normed_ref, inverse_ref, kept_ref, wide):
     pair = block_in(pair_ref)
     flat_ref[...] = pair.astype(BF16)
     pair_normed, inverse = norm_parts(pair)
@@ -278,16 +271,14 @@
 
 def turn_kernel(
     mix_ref, after_ref, gating_ref, cot_ref, out_ref, normed_ref,
-    pair_out_hbm, message_ref, cot_out_ref, gate_up_ref, gate_part_ref, out_part_ref, narrow, pair_out, sem,
+    pair_out_ref, message_ref, cot_out_ref, gate_up_ref, gate_part_ref, out_part_ref, narrow,
 ):
     (mix,) = unpack(mix_ref, narrow, 1)
     mix_normed, mix_inverse = norm_parts(mix)
     normed_mix = mix_normed.astype(BF16)
     product = dot(out_ref[1], normed_mix, 0, 0)
     gating = gating_ref[...]
-    pair_out[...] = block_out_exact((after_ref[...].astype(F32) + gating * product).astype(BF16))
-    copy = pltpu.make_async_copy(pair_out, pair_out_hbm, sem)
-    copy.start()
+    pair_out_ref[...] = (after_ref[...].astype(F32) + gating * product).astype(BF16)
     cot = block_in(cot_ref)
     cot_out_ref[...] = cot.astype(BF16)
     mix_grad, out_part, gate_up = back_head(cot, gating, product, normed_mix, mix_normed, mix_inverse, out_ref[1])
@@ -295,7 +286,6 @@
     out_part_ref[...] = out_part
     gate_up_ref[...] = gate_up
     gate_part_ref[...] = dot(normed_ref[...].astype(BF16), gate_up, 1, 1)
-    copy.wait()
 
 
 def back_kernel(
@@ -324,7 +314,7 @@
 def last_kernel(
     grads_ref, upstream_ref, normed_ref, inverse_ref, kept_ref, gate_up_ref, proj_ref, gate_ref,
     proj1_ref, gate1_ref, out1_ref, out0_ref,
-    pair_grad_hbm, message_ref, wide, pair_grad, sem,
+    pair_grad_ref, message_ref, wide,
 ):
     left_grad, right_grad = unpack(grads_ref, wide, 2)
     pair_normed = normed_ref[...]
@@ -333,9 +323,7 @@
         upstream_ref[...], pair_normed, inverse_ref[...], kept_ref, left_grad, right_grad, gate_up,
         proj_ref[0], gate_ref[0],
     )
-    pair_grad[...] = block_out(total)
-    copy = pltpu.make_async_copy(pair_grad, pair_grad_hbm, sem)
-    copy.start()
+    pair_grad_ref[...] = total
     normed = pair_normed.astype(BF16)
     proj_part = dot(normed, proj_up, 1, 1)
     parts = [proj_part[:, q * LANES : (q + 1) * LANES] for q in range(4)]
@@ -343,7 +331,6 @@
     parts += [dot(normed, gate_up, 1, 1), gate1_ref[...], out0_ref[...], out1_ref[...]]
     for q, part in enumerate(parts):
         message_ref[q * CHANNELS : (q + 1) * CHANNELS, :] = part.astype(BF16)
-    copy.wait()
 
 
 def sum_kernel(parts_ref, total_ref):
@@ -354,38 +341,51 @@
     total_ref[...] = jnp.broadcast_to(total, pairs.shape).reshape(DEVICES * WEIGHTS, LANES).astype(BF16)
 
 
-def spread_kernel(sums_ref, proj_hbm, gate_hbm, out_hbm, proj, gate, out, sems):
+def spread_kernel(
+    sums_ref, pair_out_ref, pair_grad_ref, proj_hbm, gate_hbm, out_hbm, pair_out_hbm, pair_grad_hbm,
+    proj, gate, out, pair_out, pair_grad, sems,
+):
+    copies = []
+
+    def send(source, target):
+        copies.append(pltpu.make_async_copy(source, target, sems.at[len(copies)]))
+        copies[-1].start()
+
     parts = [sums_ref[q * CHANNELS : (q + 1) * CHANNELS, :].astype(F32) for q in range(WEIGHTS)]
-    copies = []
     for l in range(2):
         proj[l] = jnp.concatenate(parts[4 * l : 4 * l + 4], axis=1)
-        copies.append(pltpu.make_async_copy(proj.at[l], proj_hbm.at[l], sems.at[l]))
-        copies[-1].start()
+        send(proj.at[l], proj_hbm.at[l])
     for l in range(2):
         gate[l], out[l] = parts[8 + l], parts[10 + l]
-    copies.append(pltpu.make_async_copy(gate, gate_hbm, sems.at[2]))
-    copies.append(pltpu.make_async_copy(out, out_hbm, sems.at[3]))
-    for copy in copies[2:]:
-        copy.start()
+    send(gate, gate_hbm)
+    send(out, out_hbm)
+    for s in range(TILES):
+        low = s * PER * COLS
+        count = min(PER * COLS, ROWS * COLS - low)
+        pair_grad[low : low + count, :] = pair_grad_ref[:, s * LANES : (s + 1) * LANES].T[:count]
+        send(pair_grad.at[pl.ds(low, count)], pair_grad_hbm.at[pl.ds(low, count)])
+    pair_out[...] = block_out_exact(pair_out_ref[...])
+    send(pair_out, pair_out_hbm)
     for copy in copies:
         copy.wait()
 
 
-def outgoing_kernel(edges_ref, mix_ref, left_ref, right_ref, forth_ref):
-    forth = first_to_second()
-    forth_ref[...] = forth
+def orders_kernel(forth_ref, back_ref):
+    forth_ref[...] = first_to_second()
+    back_ref[...] = second_to_first()
+
+
+def outgoing_kernel(edges_ref, forth_ref, mix_ref, left_ref, right_ref):
     left, right = [matrix_of(pieces) for pieces in pieces_in(edges_ref, 2)]
-    right = dot(forth, right, 1, 0).astype(BF16)
+    right = dot(forth_ref[...], right, 1, 0).astype(BF16)
     left_ref[...], right_ref[...] = left, right
     pieces_out([pieces_of(dot(left, right, 1, 1))], mix_ref)
 
 
-def incoming_kernel(edges_ref, mix_ref, left_ref, right_ref, back_ref):
-    back = second_to_first()
-    back_ref[...] = back
+def incoming_kernel(edges_ref, back_ref, mix_ref, left_ref, right_ref):
     left, right = [matrix_of(pieces) for pieces in pieces_in(edges_ref, 2)]
     left_ref[...], right_ref[...] = left, right
-    turned = dot(back, left, 1, 1).astype(BF16)
+    turned = dot(back_ref[...], left, 1, 1).astype(BF16)
     pieces_out([pieces_of(dot(turned, right, 1, 0))], mix_ref)
 
 
@@ -413,7 +413,7 @@
 DMA = pltpu.SemaphoreType.DMA
 
 
-def call(kernel, name, outs, scratch, *operands, far_out=()):
+def call(kernel, name, outs, scratch, *operands, far_out=(), flops=None):
     def spec(far):
         return pl.BlockSpec(memory_space=pl.ANY if far else pltpu.VMEM)
 
@@ -423,6 +423,7 @@
         in_specs=[spec(False) for _ in operands],
         out_specs=[spec(position in far_out) for position in range(len(outs))],
         scratch_shapes=scratch,
+        cost_estimate=flops and pl.CostEstimate(flops=flops, bytes_accessed=0, transcendentals=0),
         compiler_params=pltpu.CompilerParams(vmem_limit_bytes=24 * 1024 * 1024),
         name=name,
     )(*operands)
@@ -443,13 +444,14 @@
     cot = pair_cot.reshape(BLOCK)
     double = pltpu.VMEM(DOUBLE_SHAPE, F32)
     spaced = pltpu.VMEM((DEVICES * (SINGLE + 1), LANES), F32)
+    forth, back = call(orders_kernel, "orders", [(SQUARE, BF16), (SQUARE, BF16)], [], flops=4 * 1024**3)
     edges0, pair0, normed0, inverse0, kept0 = call(
         start_kernel, "start", [(DOUBLE_SHAPE, BF16), (FLAT, BF16), (FLAT, F32), (LINE, F32), (KEPT, F32)], [double],
-        pair, proj_weight,
-    )
-    mix0, left0, right0, forth = call(
-        outgoing_kernel, "outgoing", [(SINGLE_SHAPE, BF16), (SQUARE, BF16), (SQUARE, BF16), (SQUARE, BF16)], [],
-        exchange(edges0),
+        pair, proj_weight, forth,
+    )
+    mix0, left0, right0 = call(
+        outgoing_kernel, "outgoing", [(SINGLE_SHAPE, BF16), (SQUARE, BF16), (SQUARE, BF16)], [],
+        exchange(edges0), forth,
     )
     edges1, mix_normed0, mix_inverse0, product0, gating0, after, normed1, inverse1, kept1, gating1 = call(
         middle_kernel, "middle",
@@ -459,15 +461,14 @@
         ],
         [spaced, double], exchange(mix0), pair0, normed0, proj_weight, gate_weight, out_weight,
     )
-    mix1, left1, right1, back = call(
-        incoming_kernel, "incoming", [(SINGLE_SHAPE, BF16), (SQUARE, BF16), (SQUARE, BF16), (SQUARE, BF16)], [],
-        exchange(edges1),
+    mix1, left1, right1 = call(
+        incoming_kernel, "incoming", [(SINGLE_SHAPE, BF16), (SQUARE, BF16), (SQUARE, BF16)], [],
+        exchange(edges1), back,
     )
     pair_out, grad1, cot1, gate_up1, gate_part1, out_part1 = call(
         turn_kernel, "turn",
-        [(BLOCK, BF16), (SINGLE_SHAPE, BF16), (FLAT, BF16), (FLAT, BF16), (WEIGHT, F32), (WEIGHT, F32)],
-        [spaced, pltpu.VMEM(BLOCK, BF16), DMA],
-        exchange(mix1), after, gating1, cot, out_weight, normed1, far_out=(0,),
+        [(FLAT, BF16), (SINGLE_SHAPE, BF16), (FLAT, BF16), (FLAT, BF16), (WEIGHT, F32), (WEIGHT, F32)],
+        [spaced], exchange(mix1), after, gating1, cot, out_weight, normed1,
     )
     (grads1,) = call(
         incoming_back_kernel, "incoming_back", [(DOUBLE_SHAPE, BF16)], [], exchange(grad1), forth, left1, right1
@@ -482,16 +483,15 @@
         outgoing_back_kernel, "outgoing_back", [(DOUBLE_SHAPE, BF16)], [], exchange(grad0), back, left0, right0
     )
     pair_grad, parts = call(
-        last_kernel, "last", [(BLOCK, F32), (WEIGHTS_SHAPE, BF16)],
-        [double, pltpu.VMEM(BLOCK, F32), DMA],
+        last_kernel, "last", [(FLAT, F32), (WEIGHTS_SHAPE, BF16)], [double],
         exchange(grads0), upstream, normed0, inverse0, kept0, gate_up0, proj_weight, gate_weight,
-        proj_part1, gate_part1, out_part1, out_part0, far_out=(0,),
+        proj_part1, gate_part1, out_part1, out_part0,
     )
     (sums,) = call(sum_kernel, "sum", [(WEIGHTS_SHAPE, BF16)], [], exchange(parts))
-    proj_grad, gate_grad, out_grad = call(
-        spread_kernel, "spread", [((2,) + PROJ, F32), ((2,) + WEIGHT, F32), ((2,) + WEIGHT, F32)],
-        [pltpu.VMEM((2,) + PROJ, F32), pltpu.VMEM((2,) + WEIGHT, F32), pltpu.VMEM((2,) + WEIGHT, F32), DMA((4,))],
-        exchange(sums), far_out=(0, 1, 2),
+    outs = [((2,) + PROJ, F32), ((2,) + WEIGHT, F32), ((2,) + WEIGHT, F32), (BLOCK, BF16), (BLOCK, F32)]
+    proj_grad, gate_grad, out_grad, pair_out, pair_grad = call(
+        spread_kernel, "spread", outs, [pltpu.VMEM(shape, kind) for shape, kind in outs] + [DMA((5 + TILES,))],
+        exchange(sums), pair_out, pair_grad, far_out=range(5),
     )
     return (
         pair_out.reshape(ROWS, COLS, CHANNELS),

time: 182 us -> 180 us (0.989)
    pallas_call x11 -> x12, Pallas kernels: 11.1 us -> 10.2 us  [call(): pl.pallas_call(kernel, out_shape=[jax.ShapeDtypeStruct(shape, kind) for s...]
where the time goes in v4:
time: 180 us
  blocking collectives  168 us (93%)
  Pallas kernels  10.2 us (6%)
    all_to_all x10, blocking collectives, exchange(): lax.all_to_all(message.reshape(shape), AXES, 0, 0, tiled=True)  168 us
    pallas_call x12, Pallas kernels, call(): pl.pallas_call(kernel, out_shape=[jax.ShapeDtypeStruct(shape, kind) for s...  10.2 us

profile of v4, /device:TPU:1, one launch (start us, length us, event | category | flops | bytes accessed | tf_op | source)
XLA Modules:
  0.0 179.7 jit_solution(3464870106224678540)
XLA Ops:
  0.7 0.2 orders.1
  0.9 0.7 copy-done
  1.6 0.1 copy-done.4
  1.6 0.7 start.1
  2.4 23.7 %all_to_all.50 = bf16[128,7,2,128]{3,2,1,0:T(2,128)(2,1)S(1)} all-to-all(bf16[128,7,2,128]{3,2,1,0:T(2,128)(2,1)S(1)} %bitcast.38), channel_id=1, replica_groups=mesh['row'=16,'col'=8] {'row','col'}, dimensions={0} | all-to-all | bytes 917504 | tf_op jit(solution)/shard_map/all_to_all | solution.py:439
  26.1 1.0 outgoing.1
  27.1 15.5 %all_to_all.51 = bf16[128,8,128]{2,1,0:T(8,128)(2,1)S(1)} all-to-all(bf16[128,8,128]{2,1,0:T(8,128)(2,1)S(1)} %bitcast.42), channel_id=1, replica_groups=mesh['row'=16,'col'=8] {'row','col'}, dimensions={0} | all-to-all | bytes 524288 | tf_op jit(solution)/shard_map/all_to_all | solution.py:439
  42.6 1.1 middle.1
  43.6 16.5 %all_to_all.52 = bf16[128,7,2,128]{3,2,1,0:T(2,128)(2,1)S(1)} all-to-all(bf16[128,7,2,128]{3,2,1,0:T(2,128)(2,1)S(1)} %bitcast.37), channel_id=1, replica_groups=mesh['row'=16,'col'=8] {'row','col'}, dimensions={0} | all-to-all | bytes 917504 | tf_op jit(solution)/shard_map/all_to_all | solution.py:439
  60.2 0.9 incoming.1
  61.1 15.5 %all_to_all.53 = bf16[128,8,128]{2,1,0:T(8,128)(2,1)S(1)} all-to-all(bf16[128,8,128]{2,1,0:T(8,128)(2,1)S(1)} %bitcast.43), channel_id=1, replica_groups=mesh['row'=16,'col'=8] {'row','col'}, dimensions={0} | all-to-all | bytes 524288 | tf_op jit(solution)/shard_map/all_to_all | solution.py:439
  76.7 0.8 turn.1
  77.5 15.1 %all_to_all.54 = bf16[128,8,128]{2,1,0:T(8,128)(2,1)S(1)} all-to-all(bf16[128,8,128]{2,1,0:T(8,128)(2,1)S(1)} %bitcast.41), channel_id=1, replica_groups=mesh['row'=16,'col'=8] {'row','col'}, dimensions={0} | all-to-all | bytes 524288 | tf_op jit(solution)/shard_map/all_to_all | solution.py:439
  92.5 1.2 incoming_back.1
  93.7 16.5 %all_to_all.55 = bf16[128,7,2,128]{3,2,1,0:T(2,128)(2,1)S(1)} all-to-all(bf16[128,7,2,128]{3,2,1,0:T(2,128)(2,1)S(1)} %bitcast.28), channel_id=1, replica_groups=mesh['row'=16,'col'=8] {'row','col'}, dimensions={0} | all-to-all | bytes 917504 | tf_op jit(solution)/shard_map/all_to_all | solution.py:439
  110.3 1.0 back.1
  111.3 15.5 %all_to_all.56 = bf16[128,8,128]{2,1,0:T(8,128)(2,1)S(1)} all-to-all(bf16[128,8,128]{2,1,0:T(8,128)(2,1)S(1)} %bitcast.40), channel_id=1, replica_groups=mesh['row'=16,'col'=8] {'row','col'}, dimensions={0} | all-to-all | bytes 524288 | tf_op jit(solution)/shard_map/all_to_all | solution.py:439
  126.8 1.1 outgoing_back.1
  127.9 16.5 %all_to_all.57 = bf16[128,7,2,128]{3,2,1,0:T(2,128)(2,1)S(1)} all-to-all(bf16[128,7,2,128]{3,2,1,0:T(2,128)(2,1)S(1)} %bitcast.29), channel_id=1, replica_groups=mesh['row'=16,'col'=8] {'row','col'}, dimensions={0} | all-to-all | bytes 917504 | tf_op jit(solution)/shard_map/all_to_all | solution.py:439
  144.4 0.9 last.1
  145.3 16.5 %all_to_all.58 = bf16[128,3,4,128]{3,2,1,0:T(4,128)(2,1)S(1)} all-to-all(bf16[128,3,4,128]{3,2,1,0:T(4,128)(2,1)S(1)} %bitcast.39), channel_id=1, replica_groups=mesh['row'=16,'col'=8] {'row','col'}, dimensions={0} | all-to-all | bytes 786432 | tf_op jit(solution)/shard_map/all_to_all | solution.py:439
  161.8 0.1 sum.1
  161.9 16.4 %all_to_all.59 = bf16[128,3,4,128]{3,2,1,0:T(4,128)(2,1)S(1)} all-to-all(bf16[128,3,4,128]{3,2,1,0:T(4,128)(2,1)S(1)} %bitcast.32), channel_id=1, replica_groups=mesh['row'=16,'col'=8] {'row','col'}, dimensions={0} | all-to-all | bytes 786432 | tf_op jit(solution)/shard_map/all_to_all | solution.py:439
  178.3 1.3 spread.1
  (8 shorter events, 0.0 us)
Async XLA Ops:
  0.6 1.0 copy-start
  0.6 1.0 copy-start.4
  0.9 41.7 %copy-start.1 = (bf16[2,128,128]{2,1,0:T(8,128)(2,1)S(1)}, bf16[2,128,128]{2,1,0:T(8,128)(2,1)}, u32[]{:S(2)}) copy-start(bf16[2,128,128]{2,1,0:T(8,128)(2,1)} %gate_ref.5) | copy-start | bytes 196612
  0.9 41.7 %copy-start.2 = (bf16[2,128,128]{2,1,0:T(8,128)(2,1)S(1)}, bf16[2,128,128]{2,1,0:T(8,128)(2,1)}, u32[]{:S(2)}) copy-start(bf16[2,128,128]{2,1,0:T(8,128)(2,1)} %out_ref.5) | copy-start | bytes 196612
  42.6 34.1 %copy-start.3 = (bf16[20,40,128]{2,1,0:T(8,128)(2,1)S(1)}, bf16[20,40,128]{2,1,0:T(8,128)(2,1)}, u32[]{:S(2)}) copy-start(bf16[20,40,128]{2,1,0:T(8,128)(2,1)} %param.9) | copy-start | bytes 614404

commit v5 on v4

--- a/solution.py
+++ b/solution.py
@@ -110,7 +110,7 @@
     ]
 
 
-def pieces_in(ref, count):
+def pieces_in(ref, count, clean=()):
     values = ref[...].astype(F32).reshape(PARTS_R, -1, SUBS, LANES)
     if count == 1:
         return [[values[:, c].reshape(LANES, LANES) for c in range(PARTS_C)]]
@@ -125,7 +125,9 @@
                 piece = jnp.where(sub >= shift, piece, values[:, tile + 1])
             if shift:
                 piece = pltpu.roll(piece, SUBS - shift, 1)
-            parts[a].append(jnp.where(sub < TILES, piece, 0.0).reshape(LANES, LANES))
+            if a in clean:
+                piece = jnp.where(sub < TILES, piece, 0.0)
+            parts[a].append(piece.reshape(LANES, LANES))
     return parts
 
 
@@ -290,9 +292,12 @@
 
 def back_kernel(
     grads_ref, cot_ref, normed1_ref, inverse1_ref, kept1_ref, gate_up1_ref, mix_normed_ref, mix_inverse_ref,
-    product_ref, gating0_ref, proj_ref, gate_ref, out_ref,
-    message_ref, upstream_ref, gate_up_ref, proj_part_ref, out_part_ref, narrow, wide,
+    product_ref, gating0_ref, proj_ref, gate_ref, out_ref, pair_out_ref,
+    pair_out_hbm, message_ref, upstream_ref, gate_up_ref, proj_part_ref, out_part_ref, narrow, wide, pair_out, sem,
 ):
+    pair_out[...] = block_out_exact(pair_out_ref[...])
+    copy = pltpu.make_async_copy(pair_out, pair_out_hbm, sem)
+    copy.start()
     left_grad, right_grad = unpack(grads_ref, wide, 2)
     pair_normed = normed1_ref[...]
     upstream, proj_up = back_tail(
@@ -309,6 +314,7 @@
     pack([mix_grad], message_ref, narrow)
     out_part_ref[...] = out_part
     gate_up_ref[...] = gate_up
+    copy.wait()
 
 
 def last_kernel(
@@ -342,8 +348,7 @@
 
 
 def spread_kernel(
-    sums_ref, pair_out_ref, pair_grad_ref, proj_hbm, gate_hbm, out_hbm, pair_out_hbm, pair_grad_hbm,
-    proj, gate, out, pair_out, pair_grad, sems,
+    sums_ref, pair_grad_ref, proj_hbm, gate_hbm, out_hbm, pair_grad_hbm, proj, gate, out, pair_grad, sems,
 ):
     copies = []
 
@@ -364,8 +369,6 @@
         count = min(PER * COLS, ROWS * COLS - low)
         pair_grad[low : low + count, :] = pair_grad_ref[:, s * LANES : (s + 1) * LANES].T[:count]
         send(pair_grad.at[pl.ds(low, count)], pair_grad_hbm.at[pl.ds(low, count)])
-    pair_out[...] = block_out_exact(pair_out_ref[...])
-    send(pair_out, pair_out_hbm)
     for copy in copies:
         copy.wait()
 
@@ -383,15 +386,17 @@
 
 
 def incoming_kernel(edges_ref, back_ref, mix_ref, left_ref, right_ref):
-    left, right = [matrix_of(pieces) for pieces in pieces_in(edges_ref, 2)]
-    left_ref[...], right_ref[...] = left, right
+    left, right = [matrix_of(pieces) for pieces in pieces_in(edges_ref, 2, (0,))]
     turned = dot(back_ref[...], left, 1, 1).astype(BF16)
+    left_ref[...], right_ref[...] = turned, right
     pieces_out([pieces_of(dot(turned, right, 1, 0))], mix_ref)
 
 
-def incoming_back_kernel(grad_ref, forth_ref, left_ref, right_ref, grads_ref):
-    grad = dot(forth_ref[...], matrix_of(pieces_in(grad_ref, 1)[0]), 1, 0).astype(BF16)
-    pieces_out([pieces_of(dot(right_ref[...], grad, 1, 1)), pieces_of(dot(left_ref[...], grad, 1, 0))], grads_ref)
+def incoming_back_kernel(grad_ref, back_ref, left_ref, right_ref, grads_ref):
+    grad = matrix_of(pieces_in(grad_ref, 1)[0])
+    left_grad = dot(right_ref[...], grad, 1, 1).astype(BF16)
+    right_grad = dot(left_ref[...], grad, 0, 0)
+    pieces_out([pieces_of(dot(left_grad, back_ref[...], 1, 0)), pieces_of(right_grad)], grads_ref)
 
 
 def outgoing_back_kernel(grad_ref, back_ref, left_ref, right_ref, grads_ref):
@@ -471,13 +476,13 @@
         [spaced], exchange(mix1), after, gating1, cot, out_weight, normed1,
     )
     (grads1,) = call(
-        incoming_back_kernel, "incoming_back", [(DOUBLE_SHAPE, BF16)], [], exchange(grad1), forth, left1, right1
-    )
-    grad0, upstream, gate_up0, proj_part1, out_part0 = call(
+        incoming_back_kernel, "incoming_back", [(DOUBLE_SHAPE, BF16)], [], exchange(grad1), back, left1, right1
+    )
+    pair_out, grad0, upstream, gate_up0, proj_part1, out_part0 = call(
         back_kernel, "back",
-        [(SINGLE_SHAPE, BF16), (FLAT, F32), (FLAT, BF16), (PROJ, F32), (WEIGHT, F32)],
-        [spaced, double], exchange(grads1), cot1, normed1, inverse1, kept1, gate_up1, mix_normed0, mix_inverse0,
-        product0, gating0, proj_weight, gate_weight, out_weight,
+        [(BLOCK, BF16), (SINGLE_SHAPE, BF16), (FLAT, F32), (FLAT, BF16), (PROJ, F32), (WEIGHT, F32)],
+        [spaced, double, pltpu.VMEM(BLOCK, BF16), DMA], exchange(grads1), cot1, normed1, inverse1, kept1, gate_up1, mix_normed0, mix_inverse0,
+        product0, gating0, proj_weight, gate_weight, out_weight, pair_out, far_out=(0,),
     )
     (grads0,) = call(
         outgoing_back_kernel, "outgoing_back", [(DOUBLE_SHAPE, BF16)], [], exchange(grad0), back, left0, right0
@@ -488,10 +493,10 @@
         proj_part1, gate_part1, out_part1, out_part0,
     )
     (sums,) = call(sum_kernel, "sum", [(WEIGHTS_SHAPE, BF16)], [], exchange(parts))
-    outs = [((2,) + PROJ, F32), ((2,) + WEIGHT, F32), ((2,) + WEIGHT, F32), (BLOCK, BF16), (BLOCK, F32)]
-    proj_grad, gate_grad, out_grad, pair_out, pair_grad = call(
-        spread_kernel, "spread", outs, [pltpu.VMEM(shape, kind) for shape, kind in outs] + [DMA((5 + TILES,))],
-        exchange(sums), pair_out, pair_grad, far_out=range(5),
+    outs = [((2,) + PROJ, F32), ((2,) + WEIGHT, F32), ((2,) + WEIGHT, F32), (BLOCK, F32)]
+    proj_grad, gate_grad, out_grad, pair_grad = call(
+        spread_kernel, "spread", outs, [pltpu.VMEM(shape, kind) for shape, kind in outs] + [DMA((4 + TILES,))],
+        exchange(sums), pair_grad, far_out=range(4),
     )
     return (
         pair_out.reshape(ROWS, COLS, CHANNELS),

time: 180 us -> 180 us (level)
  no operation moved by 1% of the time
where the time goes in v5:
time: 180 us; the launch traced here: 179 us
  blocking collectives  168 us (93%)
  Pallas kernels  9.99 us (6%)
    all_to_all x10, blocking collectives, exchange(): lax.all_to_all(message.reshape(shape), AXES, 0, 0, tiled=True)  168 us
    pallas_call x12, Pallas kernels, call(): pl.pallas_call(kernel, out_shape=[jax.ShapeDtypeStruct(shape, kind) for s...  9.99 us

profile of v5, /device:TPU:1, one launch (start us, length us, event | category | flops | bytes accessed | tf_op | source)
XLA Modules:
  0.0 179.5 jit_solution(9016575369700336217)
XLA Ops:
  0.7 0.2 orders.1
  0.9 0.7 copy-done
  1.6 0.1 copy-done.4
  1.6 0.7 start.1
  2.4 23.7 %all_to_all.50 = bf16[128,7,2,128]{3,2,1,0:T(2,128)(2,1)S(1)} all-to-all(bf16[128,7,2,128]{3,2,1,0:T(2,128)(2,1)S(1)} %bitcast.38), channel_id=1, replica_groups=mesh['row'=16,'col'=8] {'row','col'}, dimensions={0} | all-to-all | bytes 917504 | tf_op jit(solution)/shard_map/all_to_all | solution.py:444
  26.1 1.0 outgoing.1
  27.0 15.5 %all_to_all.51 = bf16[128,8,128]{2,1,0:T(8,128)(2,1)S(1)} all-to-all(bf16[128,8,128]{2,1,0:T(8,128)(2,1)S(1)} %bitcast.42), channel_id=1, replica_groups=mesh['row'=16,'col'=8] {'row','col'}, dimensions={0} | all-to-all | bytes 524288 | tf_op jit(solution)/shard_map/all_to_all | solution.py:444
  42.6 1.1 middle.1
  43.6 16.5 %all_to_all.52 = bf16[128,7,2,128]{3,2,1,0:T(2,128)(2,1)S(1)} all-to-all(bf16[128,7,2,128]{3,2,1,0:T(2,128)(2,1)S(1)} %bitcast.37), channel_id=1, replica_groups=mesh['row'=16,'col'=8] {'row','col'}, dimensions={0} | all-to-all | bytes 917504 | tf_op jit(solution)/shard_map/all_to_all | solution.py:444
  60.2 0.9 incoming.1
  61.1 15.5 %all_to_all.53 = bf16[128,8,128]{2,1,0:T(8,128)(2,1)S(1)} all-to-all(bf16[128,8,128]{2,1,0:T(8,128)(2,1)S(1)} %bitcast.43), channel_id=1, replica_groups=mesh['row'=16,'col'=8] {'row','col'}, dimensions={0} | all-to-all | bytes 524288 | tf_op jit(solution)/shard_map/all_to_all | solution.py:444
  76.6 0.8 turn.1
  77.4 15.1 %all_to_all.54 = bf16[128,8,128]{2,1,0:T(8,128)(2,1)S(1)} all-to-all(bf16[128,8,128]{2,1,0:T(8,128)(2,1)S(1)} %bitcast.41), channel_id=1, replica_groups=mesh['row'=16,'col'=8] {'row','col'}, dimensions={0} | all-to-all | bytes 524288 | tf_op jit(solution)/shard_map/all_to_all | solution.py:444
  92.5 1.0 incoming_back.1
  93.6 16.5 %all_to_all.55 = bf16[128,7,2,128]{3,2,1,0:T(2,128)(2,1)S(1)} all-to-all(bf16[128,7,2,128]{3,2,1,0:T(2,128)(2,1)S(1)} %bitcast.29), channel_id=1, replica_groups=mesh['row'=16,'col'=8] {'row','col'}, dimensions={0} | all-to-all | bytes 917504 | tf_op jit(solution)/shard_map/all_to_all | solution.py:444
  110.1 1.1 back.1
  111.2 15.5 %all_to_all.56 = bf16[128,8,128]{2,1,0:T(8,128)(2,1)S(1)} all-to-all(bf16[128,8,128]{2,1,0:T(8,128)(2,1)S(1)} %bitcast.40), channel_id=1, replica_groups=mesh['row'=16,'col'=8] {'row','col'}, dimensions={0} | all-to-all | bytes 524288 | tf_op jit(solution)/shard_map/all_to_all | solution.py:444
  126.7 1.1 outgoing_back.1
  127.8 16.5 %all_to_all.57 = bf16[128,7,2,128]{3,2,1,0:T(2,128)(2,1)S(1)} all-to-all(bf16[128,7,2,128]{3,2,1,0:T(2,128)(2,1)S(1)} %bitcast.28), channel_id=1, replica_groups=mesh['row'=16,'col'=8] {'row','col'}, dimensions={0} | all-to-all | bytes 917504 | tf_op jit(solution)/shard_map/all_to_all | solution.py:444
  144.3 0.9 last.1
  145.2 16.5 %all_to_all.58 = bf16[128,3,4,128]{3,2,1,0:T(4,128)(2,1)S(1)} all-to-all(bf16[128,3,4,128]{3,2,1,0:T(4,128)(2,1)S(1)} %bitcast.39), channel_id=1, replica_groups=mesh['row'=16,'col'=8] {'row','col'}, dimensions={0} | all-to-all | bytes 786432 | tf_op jit(solution)/shard_map/all_to_all | solution.py:444
  161.7 0.1 sum.1
  161.8 16.4 %all_to_all.59 = bf16[128,3,4,128]{3,2,1,0:T(4,128)(2,1)S(1)} all-to-all(bf16[128,3,4,128]{3,2,1,0:T(4,128)(2,1)S(1)} %bitcast.31), channel_id=1, replica_groups=mesh['row'=16,'col'=8] {'row','col'}, dimensions={0} | all-to-all | bytes 786432 | tf_op jit(solution)/shard_map/all_to_all | solution.py:444
  178.2 1.1 spread.1
  (8 shorter events, 0.0 us)
Async XLA Ops:
  0.6 1.0 copy-start
  0.6 1.0 copy-start.4
  0.9 41.7 %copy-start.1 = (bf16[2,128,128]{2,1,0:T(8,128)(2,1)S(1)}, bf16[2,128,128]{2,1,0:T(8,128)(2,1)}, u32[]{:S(2)}) copy-start(bf16[2,128,128]{2,1,0:T(8,128)(2,1)} %gate_ref.5) | copy-start | bytes 196612
  0.9 41.7 %copy-start.2 = (bf16[2,128,128]{2,1,0:T(8,128)(2,1)S(1)}, bf16[2,128,128]{2,1,0:T(8,128)(2,1)}, u32[]{:S(2)}) copy-start(bf16[2,128,128]{2,1,0:T(8,128)(2,1)} %out_ref.5) | copy-start | bytes 196612
  42.6 34.1 %copy-start.3 = (bf16[20,40,128]{2,1,0:T(8,128)(2,1)S(1)}, bf16[20,40,128]{2,1,0:T(8,128)(2,1)}, u32[]{:S(2)}) copy-start(bf16[20,40,128]{2,1,0:T(8,128)(2,1)} %param.9) | copy-start | bytes 614404

commit v6 on v5

--- a/solution.py
+++ b/solution.py
@@ -92,7 +92,7 @@
             two = [wide[e * pitch : e * pitch + SINGLE, :] for e in (d, d + 1)]
             out_ref[d * SINGLE : (d + 2) * SINGLE, :] = jnp.concatenate(two, axis=0).astype(BF16)
     else:
-        out_ref[...] = wide[...].astype(BF16)
+        out_ref[...] = wide[: DEVICES * DOUBLE, :].astype(BF16)
 
 
 def unpack(ref, wide, count):
@@ -103,7 +103,7 @@
             for e in range(2):
                 wide[(d + e) * pitch : (d + e) * pitch + SINGLE, :] = two[e * SINGLE : (e + 1) * SINGLE]
     else:
-        wide[...] = ref[...].astype(F32)
+        wide[: DEVICES * DOUBLE, :] = ref[...].astype(F32)
     return [
         jnp.concatenate([wide[pl.ds(a * TILES + s, CHANNELS, stride=pitch), :] for s in range(TILES)], axis=1)
         for a in range(count)
@@ -447,8 +447,8 @@
 def local(pair_rep, proj_weight, gate_weight, out_weight, pair_cot):
     pair = pair_rep.reshape(BLOCK)
     cot = pair_cot.reshape(BLOCK)
-    double = pltpu.VMEM(DOUBLE_SHAPE, F32)
-    spaced = pltpu.VMEM((DEVICES * (SINGLE + 1), LANES), F32)
+    double = pltpu.VMEM((DEVICES * DOUBLE + 16, LANES), F32)
+    spaced = pltpu.VMEM((DEVICES * (SINGLE + 1) + 16, LANES), F32)
     forth, back = call(orders_kernel, "orders", [(SQUARE, BF16), (SQUARE, BF16)], [], flops=4 * 1024**3)
     edges0, pair0, normed0, inverse0, kept0 = call(
         start_kernel, "start", [(DOUBLE_SHAPE, BF16), (FLAT, BF16), (FLAT, F32), (LINE, F32), (KEPT, F32)], [double],

time: 180 us -> 180 us (level)
  no operation moved by 1% of the time
where the time goes in v6:
time: 180 us; the launch traced here: 179 us
  blocking collectives  168 us (93%)
  Pallas kernels  9.99 us (6%)
    all_to_all x10, blocking collectives, exchange(): lax.all_to_all(message.reshape(shape), AXES, 0, 0, tiled=True)  168 us
    pallas_call x12, Pallas kernels, call(): pl.pallas_call(kernel, out_shape=[jax.ShapeDtypeStruct(shape, kind) for s...  9.99 us

profile of v6, /device:TPU:1, one launch (start us, length us, event | category | flops | bytes accessed | tf_op | source)
XLA Modules:
  0.0 179.5 jit_solution(14464411533082220298)
XLA Ops:
  0.7 0.2 orders.1
  0.9 0.7 copy-done
  1.6 0.1 copy-done.4
  1.6 0.7 start.1
  2.4 23.7 %all_to_all.50 = bf16[128,7,2,128]{3,2,1,0:T(2,128)(2,1)S(1)} all-to-all(bf16[128,7,2,128]{3,2,1,0:T(2,128)(2,1)S(1)} %bitcast.38), channel_id=1, replica_groups=mesh['row'=16,'col'=8] {'row','col'}, dimensions={0} | all-to-all | bytes 917504 | tf_op jit(solution)/shard_map/all_to_all | solution.py:444
  26.1 1.0 outgoing.1
  27.0 15.5 %all_to_all.51 = bf16[128,8,128]{2,1,0:T(8,128)(2,1)S(1)} all-to-all(bf16[128,8,128]{2,1,0:T(8,128)(2,1)S(1)} %bitcast.42), channel_id=1, replica_groups=mesh['row'=16,'col'=8] {'row','col'}, dimensions={0} | all-to-all | bytes 524288 | tf_op jit(solution)/shard_map/all_to_all | solution.py:444
  42.6 1.1 middle.1
  43.6 16.5 %all_to_all.52 = bf16[128,7,2,128]{3,2,1,0:T(2,128)(2,1)S(1)} all-to-all(bf16[128,7,2,128]{3,2,1,0:T(2,128)(2,1)S(1)} %bitcast.37), channel_id=1, replica_groups=mesh['row'=16,'col'=8] {'row','col'}, dimensions={0} | all-to-all | bytes 917504 | tf_op jit(solution)/shard_map/all_to_all | solution.py:444
  60.2 0.9 incoming.1
  61.1 15.5 %all_to_all.53 = bf16[128,8,128]{2,1,0:T(8,128)(2,1)S(1)} all-to-all(bf16[128,8,128]{2,1,0:T(8,128)(2,1)S(1)} %bitcast.43), channel_id=1, replica_groups=mesh['row'=16,'col'=8] {'row','col'}, dimensions={0} | all-to-all | bytes 524288 | tf_op jit(solution)/shard_map/all_to_all | solution.py:444
  76.6 0.8 turn.1
  77.5 15.1 %all_to_all.54 = bf16[128,8,128]{2,1,0:T(8,128)(2,1)S(1)} all-to-all(bf16[128,8,128]{2,1,0:T(8,128)(2,1)S(1)} %bitcast.41), channel_id=1, replica_groups=mesh['row'=16,'col'=8] {'row','col'}, dimensions={0} | all-to-all | bytes 524288 | tf_op jit(solution)/shard_map/all_to_all | solution.py:444
  92.5 1.0 incoming_back.1
  93.6 16.5 %all_to_all.55 = bf16[128,7,2,128]{3,2,1,0:T(2,128)(2,1)S(1)} all-to-all(bf16[128,7,2,128]{3,2,1,0:T(2,128)(2,1)S(1)} %bitcast.29), channel_id=1, replica_groups=mesh['row'=16,'col'=8] {'row','col'}, dimensions={0} | all-to-all | bytes 917504 | tf_op jit(solution)/shard_map/all_to_all | solution.py:444
  110.1 1.1 back.1
  111.2 15.5 %all_to_all.56 = bf16[128,8,128]{2,1,0:T(8,128)(2,1)S(1)} all-to-all(bf16[128,8,128]{2,1,0:T(8,128)(2,1)S(1)} %bitcast.40), channel_id=1, replica_groups=mesh['row'=16,'col'=8] {'row','col'}, dimensions={0} | all-to-all | bytes 524288 | tf_op jit(solution)/shard_map/all_to_all | solution.py:444
  126.7 1.1 outgoing_back.1
  127.8 16.5 %all_to_all.57 = bf16[128,7,2,128]{3,2,1,0:T(2,128)(2,1)S(1)} all-to-all(bf16[128,7,2,128]{3,2,1,0:T(2,128)(2,1)S(1)} %bitcast.28), channel_id=1, replica_groups=mesh['row'=16,'col'=8] {'row','col'}, dimensions={0} | all-to-all | bytes 917504 | tf_op jit(solution)/shard_map/all_to_all | solution.py:444
  144.3 0.9 last.1
  145.2 16.5 %all_to_all.58 = bf16[128,3,4,128]{3,2,1,0:T(4,128)(2,1)S(1)} all-to-all(bf16[128,3,4,128]{3,2,1,0:T(4,128)(2,1)S(1)} %bitcast.39), channel_id=1, replica_groups=mesh['row'=16,'col'=8] {'row','col'}, dimensions={0} | all-to-all | bytes 786432 | tf_op jit(solution)/shard_map/all_to_all | solution.py:444
  161.7 0.1 sum.1
  161.8 16.4 %all_to_all.59 = bf16[128,3,4,128]{3,2,1,0:T(4,128)(2,1)S(1)} all-to-all(bf16[128,3,4,128]{3,2,1,0:T(4,128)(2,1)S(1)} %bitcast.31), channel_id=1, replica_groups=mesh['row'=16,'col'=8] {'row','col'}, dimensions={0} | all-to-all | bytes 786432 | tf_op jit(solution)/shard_map/all_to_all | solution.py:444
  178.2 1.1 spread.1
  (8 shorter events, 0.0 us)
Async XLA Ops:
  0.6 1.0 copy-start
  0.6 1.0 copy-start.4
  0.9 41.7 %copy-start.1 = (bf16[2,128,128]{2,1,0:T(8,128)(2,1)S(1)}, bf16[2,128,128]{2,1,0:T(8,128)(2,1)}, u32[]{:S(2)}) copy-start(bf16[2,128,128]{2,1,0:T(8,128)(2,1)} %gate_ref.5) | copy-start | bytes 196612
  0.9 41.7 %copy-start.2 = (bf16[2,128,128]{2,1,0:T(8,128)(2,1)S(1)}, bf16[2,128,128]{2,1,0:T(8,128)(2,1)}, u32[]{:S(2)}) copy-start(bf16[2,128,128]{2,1,0:T(8,128)(2,1)} %out_ref.5) | copy-start | bytes 196612
  42.6 34.1 %copy-start.3 = (bf16[20,40,128]{2,1,0:T(8,128)(2,1)S(1)}, bf16[20,40,128]{2,1,0:T(8,128)(2,1)}, u32[]{:S(2)}) copy-start(bf16[20,40,128]{2,1,0:T(8,128)(2,1)} %param.9) | copy-start | bytes 614404

commit v7 on v6

--- a/solution.py
+++ b/solution.py
@@ -271,23 +271,35 @@
     gating_ref[...] = sigmoid(dot(gate_ref[1], normed, 0, 0))
 
 
-def turn_kernel(
-    mix_ref, after_ref, gating_ref, cot_ref, out_ref, normed_ref,
-    pair_out_ref, message_ref, cot_out_ref, gate_up_ref, gate_part_ref, out_part_ref, narrow,
-):
+def turn_kernel(mix_ref, mix_up_ref, message_ref, normed_mix_ref, narrow):
     (mix,) = unpack(mix_ref, narrow, 1)
     mix_normed, mix_inverse = norm_parts(mix)
-    normed_mix = mix_normed.astype(BF16)
+    normed_mix_ref[...] = mix_normed.astype(BF16)
+    mix_up = mix_up_ref[...]
+    pack([mix_inverse * (mix_up - mix_normed * mean0(mix_up * mix_normed))], message_ref, narrow)
+
+
+def before_turn(cot_ref, gating_ref, out_ref, cot_flat_ref, through_ref, mix_up_ref):
+    cot = block_in(cot_ref)
+    cot_flat_ref[...] = cot.astype(BF16)
+    through = (cot * gating_ref[...]).astype(BF16)
+    through_ref[...] = through
+    mix_up = dot(out_ref[1], through, 1, 0)
+    mix_up_ref[...] = mix_up - mean0(mix_up)
+
+
+def after_turn(
+    normed_mix_ref, after_ref, gating_ref, cot_ref, through_ref, out_ref, normed_ref,
+    pair_out_ref, gate_up_ref, gate_part_ref, out_part_ref,
+):
+    normed_mix = normed_mix_ref[...]
     product = dot(out_ref[1], normed_mix, 0, 0)
     gating = gating_ref[...]
     pair_out_ref[...] = (after_ref[...].astype(F32) + gating * product).astype(BF16)
-    cot = block_in(cot_ref)
-    cot_out_ref[...] = cot.astype(BF16)
-    mix_grad, out_part, gate_up = back_head(cot, gating, product, normed_mix, mix_normed, mix_inverse, out_ref[1])
-    pack([mix_grad], message_ref, narrow)
-    out_part_ref[...] = out_part
+    gate_up = (cot_ref[...].astype(F32) * product * gating * (1.0 - gating)).astype(BF16)
     gate_up_ref[...] = gate_up
     gate_part_ref[...] = dot(normed_ref[...].astype(BF16), gate_up, 1, 1)
+    out_part_ref[...] = dot(normed_mix, through_ref[...], 1, 1)
 
 
 def back_kernel(
@@ -385,18 +397,21 @@
     pieces_out([pieces_of(dot(left, right, 1, 1))], mix_ref)
 
 
-def incoming_kernel(edges_ref, back_ref, mix_ref, left_ref, right_ref):
+def incoming_kernel(edges_ref, back_ref, cot_ref, gating_ref, out_ref, mix_ref, left_ref, right_ref, *side):
     left, right = [matrix_of(pieces) for pieces in pieces_in(edges_ref, 2, (0,))]
     turned = dot(back_ref[...], left, 1, 1).astype(BF16)
     left_ref[...], right_ref[...] = turned, right
     pieces_out([pieces_of(dot(turned, right, 1, 0))], mix_ref)
-
-
-def incoming_back_kernel(grad_ref, back_ref, left_ref, right_ref, grads_ref):
+    before_turn(cot_ref, gating_ref, out_ref, *side)
+
+
+def incoming_back_kernel(grad_ref, back_ref, left_ref, right_ref, *side):
+    *side, grads_ref = side
     grad = matrix_of(pieces_in(grad_ref, 1)[0])
     left_grad = dot(right_ref[...], grad, 1, 1).astype(BF16)
     right_grad = dot(left_ref[...], grad, 0, 0)
     pieces_out([pieces_of(dot(left_grad, back_ref[...], 1, 0)), pieces_of(right_grad)], grads_ref)
+    after_turn(*side)
 
 
 def outgoing_back_kernel(grad_ref, back_ref, left_ref, right_ref, grads_ref):
@@ -466,17 +481,18 @@
         ],
         [spaced, double], exchange(mix0), pair0, normed0, proj_weight, gate_weight, out_weight,
     )
-    mix1, left1, right1 = call(
-        incoming_kernel, "incoming", [(SINGLE_SHAPE, BF16), (SQUARE, BF16), (SQUARE, BF16)], [],
-        exchange(edges1), back,
-    )
-    pair_out, grad1, cot1, gate_up1, gate_part1, out_part1 = call(
-        turn_kernel, "turn",
-        [(FLAT, BF16), (SINGLE_SHAPE, BF16), (FLAT, BF16), (FLAT, BF16), (WEIGHT, F32), (WEIGHT, F32)],
-        [spaced], exchange(mix1), after, gating1, cot, out_weight, normed1,
-    )
-    (grads1,) = call(
-        incoming_back_kernel, "incoming_back", [(DOUBLE_SHAPE, BF16)], [], exchange(grad1), back, left1, right1
+    mix1, left1, right1, cot1, through1, mix_up1 = call(
+        incoming_kernel, "incoming",
+        [(SINGLE_SHAPE, BF16), (SQUARE, BF16), (SQUARE, BF16), (FLAT, BF16), (FLAT, BF16), (FLAT, F32)], [],
+        exchange(edges1), back, cot, gating1, out_weight,
+    )
+    grad1, normed_mix1 = call(
+        turn_kernel, "turn", [(SINGLE_SHAPE, BF16), (FLAT, BF16)], [spaced], exchange(mix1), mix_up1
+    )
+    pair_out, gate_up1, gate_part1, out_part1, grads1 = call(
+        incoming_back_kernel, "incoming_back",
+        [(FLAT, BF16), (FLAT, BF16), (WEIGHT, F32), (WEIGHT, F32), (DOUBLE_SHAPE, BF16)], [],
+        exchange(grad1), back, left1, right1, normed_mix1, after, gating1, cot1, through1, out_weight, normed1,
     )
     pair_out, grad0, upstream, gate_up0, proj_part1, out_part0 = call(
         back_kernel, "back",

time: 180 us -> 180 us (level)
  no operation moved by 1% of the time
where the time goes in v7:
time: 180 us; the launch traced here: 179 us
  blocking collectives  168 us (93%)
  Pallas kernels  9.85 us (5%)
    all_to_all x10, blocking collectives, exchange(): lax.all_to_all(message.reshape(shape), AXES, 0, 0, tiled=True)  168 us
    pallas_call x12, Pallas kernels, call(): pl.pallas_call(kernel, out_shape=[jax.ShapeDtypeStruct(shape, kind) for s...  9.85 us

profile of v7, /device:TPU:1, one launch (start us, length us, event | category | flops | bytes accessed | tf_op | source)
XLA Modules:
  0.0 179.3 jit_solution(18312795300566333437)
XLA Ops:
  0.7 0.2 orders.1
  0.9 0.7 copy-done
  1.6 0.1 copy-done.3
  1.6 0.7 start.1
  2.4 23.7 %all_to_all.50 = bf16[128,7,2,128]{3,2,1,0:T(2,128)(2,1)S(1)} all-to-all(bf16[128,7,2,128]{3,2,1,0:T(2,128)(2,1)S(1)} %bitcast.38), channel_id=1, replica_groups=mesh['row'=16,'col'=8] {'row','col'}, dimensions={0} | all-to-all | bytes 917504 | tf_op jit(solution)/shard_map/all_to_all | solution.py:459
  26.1 1.0 outgoing.1
  27.0 15.5 %all_to_all.51 = bf16[128,8,128]{2,1,0:T(8,128)(2,1)S(1)} all-to-all(bf16[128,8,128]{2,1,0:T(8,128)(2,1)S(1)} %bitcast.42), channel_id=1, replica_groups=mesh['row'=16,'col'=8] {'row','col'}, dimensions={0} | all-to-all | bytes 524288 | tf_op jit(solution)/shard_map/all_to_all | solution.py:459
  42.6 1.1 middle.1
  43.6 16.5 %all_to_all.52 = bf16[128,7,2,128]{3,2,1,0:T(2,128)(2,1)S(1)} all-to-all(bf16[128,7,2,128]{3,2,1,0:T(2,128)(2,1)S(1)} %bitcast.36), channel_id=1, replica_groups=mesh['row'=16,'col'=8] {'row','col'}, dimensions={0} | all-to-all | bytes 917504 | tf_op jit(solution)/shard_map/all_to_all | solution.py:459
  60.2 1.0 incoming.1
  61.2 15.5 %all_to_all.53 = bf16[128,8,128]{2,1,0:T(8,128)(2,1)S(1)} all-to-all(bf16[128,8,128]{2,1,0:T(8,128)(2,1)S(1)} %bitcast.41), channel_id=1, replica_groups=mesh['row'=16,'col'=8] {'row','col'}, dimensions={0} | all-to-all | bytes 524288 | tf_op jit(solution)/shard_map/all_to_all | solution.py:459
  76.7 0.4 turn.1
  77.1 15.1 %all_to_all.54 = bf16[128,8,128]{2,1,0:T(8,128)(2,1)S(1)} all-to-all(bf16[128,8,128]{2,1,0:T(8,128)(2,1)S(1)} %bitcast.43), channel_id=1, replica_groups=mesh['row'=16,'col'=8] {'row','col'}, dimensions={0} | all-to-all | bytes 524288 | tf_op jit(solution)/shard_map/all_to_all | solution.py:459
  92.1 1.3 incoming_back.1
  93.4 16.5 %all_to_all.55 = bf16[128,7,2,128]{3,2,1,0:T(2,128)(2,1)S(1)} all-to-all(bf16[128,7,2,128]{3,2,1,0:T(2,128)(2,1)S(1)} %bitcast.37), channel_id=1, replica_groups=mesh['row'=16,'col'=8] {'row','col'}, dimensions={0} | all-to-all | bytes 917504 | tf_op jit(solution)/shard_map/all_to_all | solution.py:459
  110.0 1.1 back.1
  111.1 15.5 %all_to_all.56 = bf16[128,8,128]{2,1,0:T(8,128)(2,1)S(1)} all-to-all(bf16[128,8,128]{2,1,0:T(8,128)(2,1)S(1)} %bitcast.40), channel_id=1, replica_groups=mesh['row'=16,'col'=8] {'row','col'}, dimensions={0} | all-to-all | bytes 524288 | tf_op jit(solution)/shard_map/all_to_all | solution.py:459
  126.6 1.1 outgoing_back.1
  127.6 16.5 %all_to_all.57 = bf16[128,7,2,128]{3,2,1,0:T(2,128)(2,1)S(1)} all-to-all(bf16[128,7,2,128]{3,2,1,0:T(2,128)(2,1)S(1)} %bitcast.28), channel_id=1, replica_groups=mesh['row'=16,'col'=8] {'row','col'}, dimensions={0} | all-to-all | bytes 917504 | tf_op jit(solution)/shard_map/all_to_all | solution.py:459
  144.2 0.9 last.1
  145.1 16.5 %all_to_all.58 = bf16[128,3,4,128]{3,2,1,0:T(4,128)(2,1)S(1)} all-to-all(bf16[128,3,4,128]{3,2,1,0:T(4,128)(2,1)S(1)} %bitcast.39), channel_id=1, replica_groups=mesh['row'=16,'col'=8] {'row','col'}, dimensions={0} | all-to-all | bytes 786432 | tf_op jit(solution)/shard_map/all_to_all | solution.py:459
  161.6 0.1 sum.1
  161.7 16.4 %all_to_all.59 = bf16[128,3,4,128]{3,2,1,0:T(4,128)(2,1)S(1)} all-to-all(bf16[128,3,4,128]{3,2,1,0:T(4,128)(2,1)S(1)} %bitcast.30), channel_id=1, replica_groups=mesh['row'=16,'col'=8] {'row','col'}, dimensions={0} | all-to-all | bytes 786432 | tf_op jit(solution)/shard_map/all_to_all | solution.py:459
  178.1 1.1 spread.1
  (8 shorter events, 0.0 us)
Async XLA Ops:
  0.6 1.0 copy-start
  0.6 1.0 copy-start.3
  0.9 41.7 %copy-start.1 = (bf16[2,128,128]{2,1,0:T(8,128)(2,1)S(1)}, bf16[2,128,128]{2,1,0:T(8,128)(2,1)}, u32[]{:S(2)}) copy-start(bf16[2,128,128]{2,1,0:T(8,128)(2,1)} %out_ref.5) | copy-start | bytes 196612
  0.9 41.7 %copy-start.2 = (bf16[2,128,128]{2,1,0:T(8,128)(2,1)S(1)}, bf16[2,128,128]{2,1,0:T(8,128)(2,1)}, u32[]{:S(2)}) copy-start(bf16[2,128,128]{2,1,0:T(8,128)(2,1)} %gate_ref.5) | copy-start | bytes 196612
  26.1 34.1 %copy-start.4 = (bf16[20,40,128]{2,1,0:T(8,128)(2,1)S(1)}, bf16[20,40,128]{2,1,0:T(8,128)(2,1)}, u32[]{:S(2)}) copy-start(bf16[20,40,128]{2,1,0:T(8,128)(2,1)} %param.9) | copy-start | bytes 614404

commit v8 on v7

--- a/solution.py
+++ b/solution.py
@@ -249,8 +249,8 @@
 
 
 def middle_kernel(
-    mix_ref, pair_ref, normed0_ref, proj_ref, gate_ref, out_ref,
-    message_ref, mix_normed_ref, mix_inverse_ref, product_ref, gating0_ref, after_ref, normed_ref, inverse_ref, kept_ref,
+    mix_ref, pair_ref, gating0_ref, proj_ref, gate_ref, out_ref,
+    message_ref, mix_normed_ref, mix_inverse_ref, product_ref, after_ref, normed_ref, inverse_ref, kept_ref,
     gating_ref, narrow, wide,
 ):
     (mix,) = unpack(mix_ref, narrow, 1)
@@ -259,9 +259,7 @@
     mix_inverse_ref[...] = mix_inverse
     product = dot(out_ref[0], mix_normed.astype(BF16), 0, 0)
     product_ref[...] = product
-    gating0 = sigmoid(dot(gate_ref[0], normed0_ref[...].astype(BF16), 0, 0))
-    gating0_ref[...] = gating0
-    after = (pair_ref[...].astype(F32) + gating0 * product).astype(BF16)
+    after = (pair_ref[...].astype(F32) + gating0_ref[...] * product).astype(BF16)
     after_ref[...] = after
     pair_normed, inverse = norm_parts(after.astype(F32))
     normed_ref[...] = pair_normed
@@ -390,11 +388,12 @@
     back_ref[...] = second_to_first()
 
 
-def outgoing_kernel(edges_ref, forth_ref, mix_ref, left_ref, right_ref):
+def outgoing_kernel(edges_ref, forth_ref, normed_ref, gate_ref, mix_ref, left_ref, right_ref, gating_ref):
     left, right = [matrix_of(pieces) for pieces in pieces_in(edges_ref, 2)]
     right = dot(forth_ref[...], right, 1, 0).astype(BF16)
     left_ref[...], right_ref[...] = left, right
     pieces_out([pieces_of(dot(left, right, 1, 1))], mix_ref)
+    gating_ref[...] = sigmoid(dot(gate_ref[0], normed_ref[...].astype(BF16), 0, 0))
 
 
 def incoming_kernel(edges_ref, back_ref, cot_ref, gating_ref, out_ref, mix_ref, left_ref, right_ref, *side):
@@ -469,17 +468,17 @@
         start_kernel, "start", [(DOUBLE_SHAPE, BF16), (FLAT, BF16), (FLAT, F32), (LINE, F32), (KEPT, F32)], [double],
         pair, proj_weight, forth,
     )
-    mix0, left0, right0 = call(
-        outgoing_kernel, "outgoing", [(SINGLE_SHAPE, BF16), (SQUARE, BF16), (SQUARE, BF16)], [],
-        exchange(edges0), forth,
-    )
-    edges1, mix_normed0, mix_inverse0, product0, gating0, after, normed1, inverse1, kept1, gating1 = call(
+    mix0, left0, right0, gating0 = call(
+        outgoing_kernel, "outgoing", [(SINGLE_SHAPE, BF16), (SQUARE, BF16), (SQUARE, BF16), (FLAT, F32)], [],
+        exchange(edges0), forth, normed0, gate_weight,
+    )
+    edges1, mix_normed0, mix_inverse0, product0, after, normed1, inverse1, kept1, gating1 = call(
         middle_kernel, "middle",
         [
-            (DOUBLE_SHAPE, BF16), (FLAT, F32), (LINE, F32), (FLAT, F32), (FLAT, F32), (FLAT, BF16), (FLAT, F32),
+            (DOUBLE_SHAPE, BF16), (FLAT, F32), (LINE, F32), (FLAT, F32), (FLAT, BF16), (FLAT, F32),
             (LINE, F32), (KEPT, F32), (FLAT, F32),
         ],
-        [spaced, double], exchange(mix0), pair0, normed0, proj_weight, gate_weight, out_weight,
+        [spaced, double], exchange(mix0), pair0, gating0, proj_weight, gate_weight, out_weight,
     )
     mix1, left1, right1, cot1, through1, mix_up1 = call(
         incoming_kernel, "incoming",

time: 180 us -> 180 us (level)
  no operation moved by 1% of the time
where the time goes in v8:
time: 180 us; the launch traced here: 179 us
  blocking collectives  168 us (93%)
  Pallas kernels  9.73 us (5%)
    all_to_all x10, blocking collectives, exchange(): lax.all_to_all(message.reshape(shape), AXES, 0, 0, tiled=True)  168 us
    pallas_call x12, Pallas kernels, call(): pl.pallas_call(kernel, out_shape=[jax.ShapeDtypeStruct(shape, kind) for s...  9.73 us

profile of v8, /device:TPU:1, one launch (start us, length us, event | category | flops | bytes accessed | tf_op | source)
XLA Modules:
  0.0 179.2 jit_solution(17174142786707356523)
XLA Ops:
  0.7 0.2 orders.1
  0.9 0.7 copy-done
  1.6 0.1 copy-done.3
  1.6 0.7 start.1
  2.4 23.7 %all_to_all.50 = bf16[128,7,2,128]{3,2,1,0:T(2,128)(2,1)S(1)} all-to-all(bf16[128,7,2,128]{3,2,1,0:T(2,128)(2,1)S(1)} %bitcast.38), channel_id=1, replica_groups=mesh['row'=16,'col'=8] {'row','col'}, dimensions={0} | all-to-all | bytes 917504 | tf_op jit(solution)/shard_map/all_to_all | solution.py:458
  26.1 1.0 outgoing.1
  27.1 15.5 %all_to_all.51 = bf16[128,8,128]{2,1,0:T(8,128)(2,1)S(1)} all-to-all(bf16[128,8,128]{2,1,0:T(8,128)(2,1)S(1)} %bitcast.42), channel_id=1, replica_groups=mesh['row'=16,'col'=8] {'row','col'}, dimensions={0} | all-to-all | bytes 524288 | tf_op jit(solution)/shard_map/all_to_all | solution.py:458
  42.6 0.9 middle.1
  43.5 16.5 %all_to_all.52 = bf16[128,7,2,128]{3,2,1,0:T(2,128)(2,1)S(1)} all-to-all(bf16[128,7,2,128]{3,2,1,0:T(2,128)(2,1)S(1)} %bitcast.37), channel_id=1, replica_groups=mesh['row'=16,'col'=8] {'row','col'}, dimensions={0} | all-to-all | bytes 917504 | tf_op jit(solution)/shard_map/all_to_all | solution.py:458
  60.1 1.0 incoming.1
  61.1 15.5 %all_to_all.53 = bf16[128,8,128]{2,1,0:T(8,128)(2,1)S(1)} all-to-all(bf16[128,8,128]{2,1,0:T(8,128)(2,1)S(1)} %bitcast.41), channel_id=1, replica_groups=mesh['row'=16,'col'=8] {'row','col'}, dimensions={0} | all-to-all | bytes 524288 | tf_op jit(solution)/shard_map/all_to_all | solution.py:458
  76.6 0.4 turn.1
  77.0 15.1 %all_to_all.54 = bf16[128,8,128]{2,1,0:T(8,128)(2,1)S(1)} all-to-all(bf16[128,8,128]{2,1,0:T(8,128)(2,1)S(1)} %bitcast.43), channel_id=1, replica_groups=mesh['row'=16,'col'=8] {'row','col'}, dimensions={0} | all-to-all | bytes 524288 | tf_op jit(solution)/shard_map/all_to_all | solution.py:458
  92.0 1.3 incoming_back.1
  93.3 16.5 %all_to_all.55 = bf16[128,7,2,128]{3,2,1,0:T(2,128)(2,1)S(1)} all-to-all(bf16[128,7,2,128]{3,2,1,0:T(2,128)(2,1)S(1)} %bitcast.36), channel_id=1, replica_groups=mesh['row'=16,'col'=8] {'row','col'}, dimensions={0} | all-to-all | bytes 917504 | tf_op jit(solution)/shard_map/all_to_all | solution.py:458
  109.9 1.1 back.1
  111.0 15.5 %all_to_all.56 = bf16[128,8,128]{2,1,0:T(8,128)(2,1)S(1)} all-to-all(bf16[128,8,128]{2,1,0:T(8,128)(2,1)S(1)} %bitcast.40), channel_id=1, replica_groups=mesh['row'=16,'col'=8] {'row','col'}, dimensions={0} | all-to-all | bytes 524288 | tf_op jit(solution)/shard_map/all_to_all | solution.py:458
  126.5 1.1 outgoing_back.1
  127.5 16.5 %all_to_all.57 = bf16[128,7,2,128]{3,2,1,0:T(2,128)(2,1)S(1)} all-to-all(bf16[128,7,2,128]{3,2,1,0:T(2,128)(2,1)S(1)} %bitcast.28), channel_id=1, replica_groups=mesh['row'=16,'col'=8] {'row','col'}, dimensions={0} | all-to-all | bytes 917504 | tf_op jit(solution)/shard_map/all_to_all | solution.py:458
  144.1 0.9 last.1
  145.0 16.5 %all_to_all.58 = bf16[128,3,4,128]{3,2,1,0:T(4,128)(2,1)S(1)} all-to-all(bf16[128,3,4,128]{3,2,1,0:T(4,128)(2,1)S(1)} %bitcast.39), channel_id=1, replica_groups=mesh['row'=16,'col'=8] {'row','col'}, dimensions={0} | all-to-all | bytes 786432 | tf_op jit(solution)/shard_map/all_to_all | solution.py:458
  161.5 0.1 sum.1
  161.6 16.4 %all_to_all.59 = bf16[128,3,4,128]{3,2,1,0:T(4,128)(2,1)S(1)} all-to-all(bf16[128,3,4,128]{3,2,1,0:T(4,128)(2,1)S(1)} %bitcast.30), channel_id=1, replica_groups=mesh['row'=16,'col'=8] {'row','col'}, dimensions={0} | all-to-all | bytes 786432 | tf_op jit(solution)/shard_map/all_to_all | solution.py:458
  177.9 1.1 spread.1
  (8 shorter events, 0.0 us)
Async XLA Ops:
  0.6 1.0 copy-start
  0.6 1.0 copy-start.3
  0.7 25.4 %copy-start.1 = (bf16[2,128,128]{2,1,0:T(8,128)(2,1)S(1)}, bf16[2,128,128]{2,1,0:T(8,128)(2,1)}, u32[]{:S(2)}) copy-start(bf16[2,128,128]{2,1,0:T(8,128)(2,1)} %gate_ref.7) | copy-start | bytes 196612
  0.9 41.7 %copy-start.2 = (bf16[2,128,128]{2,1,0:T(8,128)(2,1)S(1)}, bf16[2,128,128]{2,1,0:T(8,128)(2,1)}, u32[]{:S(2)}) copy-start(bf16[2,128,128]{2,1,0:T(8,128)(2,1)} %out_ref.5) | copy-start | bytes 196612
  26.1 34.0 %copy-start.4 = (bf16[20,40,128]{2,1,0:T(8,128)(2,1)S(1)}, bf16[20,40,128]{2,1,0:T(8,128)(2,1)}, u32[]{:S(2)}) copy-start(bf16[20,40,128]{2,1,0:T(8,128)(2,1)} %param.9) | copy-start | bytes 614404

commit v9 on v8

--- a/solution.py
+++ b/solution.py
@@ -239,9 +239,8 @@
     return upstream + norm_back(pair_normed, pair_inverse, normed_up), proj_up
 
 
-def start_kernel(pair_ref, proj_ref, _, message_ref, flat_ref, normed_ref, inverse_ref, kept_ref, wide):
+def start_kernel(pair_ref, proj_ref, _, message_ref, normed_ref, inverse_ref, kept_ref, wide):
     pair = block_in(pair_ref)
-    flat_ref[...] = pair.astype(BF16)
     pair_normed, inverse = norm_parts(pair)
     normed_ref[...] = pair_normed
     inverse_ref[...] = inverse
@@ -388,12 +387,13 @@
     back_ref[...] = second_to_first()
 
 
-def outgoing_kernel(edges_ref, forth_ref, normed_ref, gate_ref, mix_ref, left_ref, right_ref, gating_ref):
+def outgoing_kernel(edges_ref, forth_ref, normed_ref, gate_ref, pair_ref, mix_ref, left_ref, right_ref, gating_ref, flat_ref):
     left, right = [matrix_of(pieces) for pieces in pieces_in(edges_ref, 2)]
     right = dot(forth_ref[...], right, 1, 0).astype(BF16)
     left_ref[...], right_ref[...] = left, right
     pieces_out([pieces_of(dot(left, right, 1, 1))], mix_ref)
     gating_ref[...] = sigmoid(dot(gate_ref[0], normed_ref[...].astype(BF16), 0, 0))
+    flat_ref[...] = block_in(pair_ref).astype(BF16)
 
 
 def incoming_kernel(edges_ref, back_ref, cot_ref, gating_ref, out_ref, mix_ref, left_ref, right_ref, *side):
@@ -464,13 +464,13 @@
     double = pltpu.VMEM((DEVICES * DOUBLE + 16, LANES), F32)
     spaced = pltpu.VMEM((DEVICES * (SINGLE + 1) + 16, LANES), F32)
     forth, back = call(orders_kernel, "orders", [(SQUARE, BF16), (SQUARE, BF16)], [], flops=4 * 1024**3)
-    edges0, pair0, normed0, inverse0, kept0 = call(
-        start_kernel, "start", [(DOUBLE_SHAPE, BF16), (FLAT, BF16), (FLAT, F32), (LINE, F32), (KEPT, F32)], [double],
+    edges0, normed0, inverse0, kept0 = call(
+        start_kernel, "start", [(DOUBLE_SHAPE, BF16), (FLAT, F32), (LINE, F32), (KEPT, F32)], [double],
         pair, proj_weight, forth,
     )
-    mix0, left0, right0, gating0 = call(
-        outgoing_kernel, "outgoing", [(SINGLE_SHAPE, BF16), (SQUARE, BF16), (SQUARE, BF16), (FLAT, F32)], [],
-        exchange(edges0), forth, normed0, gate_weight,
+    mix0, left0, right0, gating0, pair0 = call(
+        outgoing_kernel, "outgoing", [(SINGLE_SHAPE, BF16), (SQUARE, BF16), (SQUARE, BF16), (FLAT, F32), (FLAT, BF16)], [],
+        exchange(edges0), forth, normed0, gate_weight, pair,
     )
     edges1, mix_normed0, mix_inverse0, product0, after, normed1, inverse1, kept1, gating1 = call(
         middle_kernel, "middle",

time: 180 us -> 180 us (level)
  no operation moved by 1% of the time
where the time goes in v9:
time: 180 us; the launch traced here: 179 us
  blocking collectives  168 us (93%)
  Pallas kernels  9.72 us (5%)
    all_to_all x10, blocking collectives, exchange(): lax.all_to_all(message.reshape(shape), AXES, 0, 0, tiled=True)  168 us
    pallas_call x12, Pallas kernels, call(): pl.pallas_call(kernel, out_shape=[jax.ShapeDtypeStruct(shape, kind) for s...  9.72 us

profile of v9, /device:TPU:1, one launch (start us, length us, event | category | flops | bytes accessed | tf_op | source)
XLA Modules:
  0.0 179.2 jit_solution(11250857710663435731)
XLA Ops:
  0.7 0.2 orders.1
  0.9 0.7 copy-done
  1.6 0.1 copy-done.3
  1.6 0.7 start.1
  2.4 23.7 %all_to_all.50 = bf16[128,7,2,128]{3,2,1,0:T(2,128)(2,1)S(1)} all-to-all(bf16[128,7,2,128]{3,2,1,0:T(2,128)(2,1)S(1)} %bitcast.40), channel_id=1, replica_groups=mesh['row'=16,'col'=8] {'row','col'}, dimensions={0} | all-to-all | bytes 917504 | tf_op jit(solution)/shard_map/all_to_all | solution.py:458
  26.1 1.0 outgoing.1
  27.1 15.5 %all_to_all.51 = bf16[128,8,128]{2,1,0:T(8,128)(2,1)S(1)} all-to-all(bf16[128,8,128]{2,1,0:T(8,128)(2,1)S(1)} %bitcast.43), channel_id=1, replica_groups=mesh['row'=16,'col'=8] {'row','col'}, dimensions={0} | all-to-all | bytes 524288 | tf_op jit(solution)/shard_map/all_to_all | solution.py:458
  42.6 0.9 middle.1
  43.5 16.5 %all_to_all.52 = bf16[128,7,2,128]{3,2,1,0:T(2,128)(2,1)S(1)} all-to-all(bf16[128,7,2,128]{3,2,1,0:T(2,128)(2,1)S(1)} %bitcast.39), channel_id=1, replica_groups=mesh['row'=16,'col'=8] {'row','col'}, dimensions={0} | all-to-all | bytes 917504 | tf_op jit(solution)/shard_map/all_to_all | solution.py:458
  60.0 1.0 incoming.1
  61.1 15.5 %all_to_all.53 = bf16[128,8,128]{2,1,0:T(8,128)(2,1)S(1)} all-to-all(bf16[128,8,128]{2,1,0:T(8,128)(2,1)S(1)} %bitcast.44), channel_id=1, replica_groups=mesh['row'=16,'col'=8] {'row','col'}, dimensions={0} | all-to-all | bytes 524288 | tf_op jit(solution)/shard_map/all_to_all | solution.py:458
  76.6 0.4 turn.1
  77.0 15.1 %all_to_all.54 = bf16[128,8,128]{2,1,0:T(8,128)(2,1)S(1)} all-to-all(bf16[128,8,128]{2,1,0:T(8,128)(2,1)S(1)} %bitcast.45), channel_id=1, replica_groups=mesh['row'=16,'col'=8] {'row','col'}, dimensions={0} | all-to-all | bytes 524288 | tf_op jit(solution)/shard_map/all_to_all | solution.py:458
  92.0 1.3 incoming_back.1
  93.3 16.5 %all_to_all.55 = bf16[128,7,2,128]{3,2,1,0:T(2,128)(2,1)S(1)} all-to-all(bf16[128,7,2,128]{3,2,1,0:T(2,128)(2,1)S(1)} %bitcast.38), channel_id=1, replica_groups=mesh['row'=16,'col'=8] {'row','col'}, dimensions={0} | all-to-all | bytes 917504 | tf_op jit(solution)/shard_map/all_to_all | solution.py:458
  109.9 1.1 back.1
  111.0 15.5 %all_to_all.56 = bf16[128,8,128]{2,1,0:T(8,128)(2,1)S(1)} all-to-all(bf16[128,8,128]{2,1,0:T(8,128)(2,1)S(1)} %bitcast.42), channel_id=1, replica_groups=mesh['row'=16,'col'=8] {'row','col'}, dimensions={0} | all-to-all | bytes 524288 | tf_op jit(solution)/shard_map/all_to_all | solution.py:458
  126.5 1.1 outgoing_back.1
  127.5 16.5 %all_to_all.57 = bf16[128,7,2,128]{3,2,1,0:T(2,128)(2,1)S(1)} all-to-all(bf16[128,7,2,128]{3,2,1,0:T(2,128)(2,1)S(1)} %bitcast.28), channel_id=1, replica_groups=mesh['row'=16,'col'=8] {'row','col'}, dimensions={0} | all-to-all | bytes 917504 | tf_op jit(solution)/shard_map/all_to_all | solution.py:458
  144.1 0.9 last.1
  145.0 16.5 %all_to_all.58 = bf16[128,3,4,128]{3,2,1,0:T(4,128)(2,1)S(1)} all-to-all(bf16[128,3,4,128]{3,2,1,0:T(4,128)(2,1)S(1)} %bitcast.41), channel_id=1, replica_groups=mesh['row'=16,'col'=8] {'row','col'}, dimensions={0} | all-to-all | bytes 786432 | tf_op jit(solution)/shard_map/all_to_all | solution.py:458
  161.5 0.1 sum.1
  161.6 16.4 %all_to_all.59 = bf16[128,3,4,128]{3,2,1,0:T(4,128)(2,1)S(1)} all-to-all(bf16[128,3,4,128]{3,2,1,0:T(4,128)(2,1)S(1)} %bitcast.30), channel_id=1, replica_groups=mesh['row'=16,'col'=8] {'row','col'}, dimensions={0} | all-to-all | bytes 786432 | tf_op jit(solution)/shard_map/all_to_all | solution.py:458
  177.9 1.1 spread.1
  (8 shorter events, 0.0 us)
Async XLA Ops:
  0.6 1.0 copy-start
  0.6 1.0 copy-start.3
  0.7 25.4 %copy-start.1 = (bf16[2,128,128]{2,1,0:T(8,128)(2,1)S(1)}, bf16[2,128,128]{2,1,0:T(8,128)(2,1)}, u32[]{:S(2)}) copy-start(bf16[2,128,128]{2,1,0:T(8,128)(2,1)} %gate_ref.7) | copy-start | bytes 196612
  1.6 40.9 %copy-start.2 = (bf16[2,128,128]{2,1,0:T(8,128)(2,1)S(1)}, bf16[2,128,128]{2,1,0:T(8,128)(2,1)}, u32[]{:S(2)}) copy-start(bf16[2,128,128]{2,1,0:T(8,128)(2,1)} %out_ref.5) | copy-start | bytes 196612
  26.1 34.0 %copy-start.4 = (bf16[20,40,128]{2,1,0:T(8,128)(2,1)S(1)}, bf16[20,40,128]{2,1,0:T(8,128)(2,1)}, u32[]{:S(2)}) copy-start(bf16[20,40,128]{2,1,0:T(8,128)(2,1)} %param.9) | copy-start | bytes 614404
